TPU v7x, 128 devices: a whole 4x4x4 slice. The times are simulated.
128 devices in a mesh: seq: 16 (over z, x), tp: 4 (over y), grp: 2 (over core).
Axes of the slice: x: 4, y: 4, z: 4, core: 2. Of those that a mesh axis runs over, the one named last changes fastest.
Arguments:
- group_hidden: bfloat16 [4, 512, 7168], P(None, 'seq', ('tp', 'grp')), may hold values from -6 to 6
- group_query: bfloat16 [4, 512, 128, 576], P(None, 'seq', ('tp', 'grp')), may hold values from -36 to 36
- past_cache: bfloat16 [4, 3072, 576], P(None, 'seq'), may hold values from -6 to 6
- past_len: int32 [4], replicated, may hold values from 1536 to 3072, as said below
- decode_hidden: bfloat16 [256, 2, 7168], P('seq', None, ('tp', 'grp')), may hold values from -6 to 6
- decode_query: bfloat16 [256, 2, 128, 576], P('seq', None, ('tp', 'grp')), may hold values from -36 to 36
- decode_pool: bfloat16 [512, 384, 576], P('seq'), may hold values from -6 to 6
- owner: int32 [256, 1], P('seq'), may hold values from 0 to 15; in each aligned block of 16 rows (0 to 15, 16 to 31, ...) at most 2 rows name the same one
- dec_len: int32 [256], P('seq'), may hold values from 1 to 382, as said below
- w_latent: bfloat16 [7168, 576], P(('tp', 'grp')), may hold values from -0.0625 to 0.0625
- kv_gain: float32 [512], replicated, may hold values from 0.5 to 1.5
- w_value: bfloat16 [128, 512, 128], P(('tp', 'grp')), may hold values from -0.25 to 0.25
Outputs:
- prefill_out: bfloat16 [4, 512, 128, 128], P(None, 'seq', ('tp', 'grp'))
- decode_out: bfloat16 [256, 2, 128, 128], P('seq', None, ('tp', 'grp'))
Inputs may be any that keep to these rules, and one draw needn't show every extreme that they name: `past_len`: at least half of the earlier positions are cached; some prompt has all 3072. `dec_len`: leaves room for the two new rows; some request has 382. Among the 16 requests that arrive at one index of seq, at most 2 name the same owner.
All inputs are finite; a program needn't handle non-finite values.
Results may differ from a plain program's by a relative error of at most 0.02.
Values may be sent and summed in bfloat16 or wider, within the bound.
No kernel may reach another device: no remote copies, remote signals or barrier semaphores. Data moves between devices by JAX's collectives and lax.ppermute only.
A program may use at most 192 MiB of HBM per device.

v0:
```python
import jax
import jax.numpy as jnp
from jax import lax
from jax.sharding import PartitionSpec as P

epsilon = 1e-06
negative = -1e30


def rotate(rope_part, positions):
    half_width = rope_part.shape[-1] // 2
    frequency = jnp.exp(-jnp.log(10000.0) * jnp.arange(half_width).astype(jnp.float32) / half_width)
    angles = positions.astype(jnp.float32)[..., None] * frequency
    cosine = jnp.cos(angles)
    sine_part = jnp.sin(angles)
    former = rope_part[..., :half_width]
    latter = rope_part[..., half_width:]
    return jnp.concatenate(
        [former * cosine - latter * sine_part, latter * cosine + former * sine_part], axis=-1
    )


def make_rows(latent, kv_gain, positions):
    lat_width = kv_gain.shape[0]
    latent_part = latent[..., :lat_width]
    spread = jnp.mean(latent_part * latent_part, axis=-1, keepdims=True)
    normed = latent_part * lax.rsqrt(spread + epsilon) * kv_gain
    return jnp.concatenate([normed, rotate(latent[..., lat_width:], positions)], axis=-1).astype(
        jnp.bfloat16
    )


def block_state(scores, allowed, values):
    masked = jnp.where(allowed, scores, negative)
    highest = jnp.max(masked, axis=-1)
    weights = jnp.where(allowed, jnp.exp(masked - highest[..., None]), 0.0)
    totals = jnp.sum(weights, axis=-1)
    summed = jnp.einsum(
        "...qk,...kc->...qc",
        weights.astype(jnp.bfloat16),
        values,
        preferred_element_type=jnp.float32,
    )
    return (highest, totals, summed)


def merge_state(former, latter):
    highest = jnp.maximum(former[0], latter[0])
    former_scale = jnp.exp(former[0] - highest)
    latter_scale = jnp.exp(latter[0] - highest)
    totals = former[1] * former_scale + latter[1] * latter_scale
    summed = former[2] * former_scale[..., None] + latter[2] * latter_scale[..., None]
    return (highest, totals, summed)


def empty_state(leading, lat_width):
    return (
        jnp.full(leading, negative, jnp.float32),
        jnp.zeros(leading, jnp.float32),
        jnp.zeros(leading + (lat_width,), jnp.float32),
    )


def on_device(
    group_hidden,
    group_query,
    past_cache,
    past_len,
    decode_hidden,
    decode_query,
    decode_pool,
    owner,
    dec_len,
    w_latent,
    kv_gain,
    w_value,
):
    seq_count = lax.axis_size("seq")
    seq_place = lax.axis_index("seq")
    prompt_count, group_local, head_local, row_width = group_query.shape
    past_local = past_cache.shape[1]
    rows_local = past_local + group_local
    request_local = decode_query.shape[0]
    lat_width = kv_gain.shape[0]
    value_width = w_value.shape[2]
    slot_count = decode_pool.shape[0]
    pair_limit = slot_count // seq_count
    cache_length = decode_pool.shape[1]
    query_pairs = 2 * head_local
    scale = (value_width + row_width - lat_width) ** (-0.5)
    group_latent = jnp.einsum(
        "ptd,dc->ptc", group_hidden, w_latent, preferred_element_type=jnp.float32
    )
    decode_latent = jnp.einsum(
        "rsd,dc->rsc", decode_hidden, w_latent, preferred_element_type=jnp.float32
    )
    group_latent, decode_latent = (
        lax.psum(group_latent.astype(jnp.bfloat16), ("tp", "grp")).astype(jnp.float32),
        lax.psum(decode_latent.astype(jnp.bfloat16), ("tp", "grp")).astype(jnp.float32),
    )
    token_local = jnp.arange(group_local, dtype=jnp.int32)
    group_positions = past_len[:, None] + seq_place * group_local + token_local[None, :]
    group_rows = make_rows(group_latent, kv_gain, group_positions)
    step_pair = jnp.arange(2, dtype=jnp.int32)
    decode_positions = past_len[0] + group_local * seq_count + dec_len[:, None] + step_pair[None, :]
    decode_rows = make_rows(decode_latent, kv_gain, decode_positions)
    local_rows = jnp.concatenate([past_cache, group_rows], axis=1)

    def row_kinds(count):
        global_row = jnp.arange(count, dtype=jnp.int32)
        holder = global_row // rows_local
        within = global_row % rows_local
        is_past = within < past_local
        past_index = holder * past_local + within
        group_index = holder * group_local + within - past_local
        return (is_past, past_index, group_index)

    group_flat = group_query.reshape(prompt_count, group_local * head_local, row_width)
    query_token = (
        seq_place * group_local
        + jnp.arange(group_local * head_local, dtype=jnp.int32) // head_local
    )
    prefill_init = empty_state((prompt_count, group_local * head_local), lat_width)
    shard_rows = lax.all_gather(local_rows, "seq", axis=1, tiled=True)
    is_past, past_index, group_index = row_kinds(shard_rows.shape[1])
    allowed = jnp.where(
        is_past[None, None, :],
        past_index[None, None, :] < past_len[:, None, None],
        group_index[None, None, :] <= query_token[None, :, None],
    )
    scores = (
        jnp.einsum("pqc,pkc->pqk", group_flat, shard_rows, preferred_element_type=jnp.float32)
        * scale
    )
    prefill_final = merge_state(
        prefill_init, block_state(scores, allowed, shard_rows[:, :, :lat_width])
    )
    prefill_latent = (prefill_final[2] / prefill_final[1][..., None]).astype(jnp.bfloat16)
    prefill_latent = prefill_latent.reshape(prompt_count, group_local, head_local, lat_width)
    prefill_out = jnp.einsum(
        "pthc,hcv->pthv", prefill_latent, w_value, preferred_element_type=jnp.float32
    ).astype(jnp.bfloat16)
    targets = owner[:, 0]
    request_order = jnp.arange(request_local, dtype=jnp.int32)
    earlier = (targets[:, None] == targets[None, :]) & (
        request_order[None, :] < request_order[:, None]
    )
    slot_rank = jnp.sum(earlier.astype(jnp.int32), axis=1)
    destination = targets * pair_limit + slot_rank
    dispatch = jnp.arange(slot_count, dtype=jnp.int32)[:, None] == destination[None, :]
    dispatch_half = dispatch.astype(jnp.bfloat16)
    send_query = jnp.dot(
        dispatch_half, decode_query.reshape(request_local, -1), preferred_element_type=jnp.float32
    ).astype(jnp.bfloat16)
    send_rows = jnp.dot(
        dispatch_half, decode_rows.reshape(request_local, -1), preferred_element_type=jnp.float32
    ).astype(jnp.bfloat16)
    send_length = jnp.sum(jnp.where(dispatch, dec_len[None, :], 0), axis=1)
    arrived_query, arrived_rows = (
        lax.all_to_all(
            send_query.reshape(seq_count, pair_limit, -1),
            "seq",
            split_axis=0,
            concat_axis=0,
            tiled=True,
        ),
        lax.all_to_all(
            send_rows.reshape(seq_count, pair_limit, -1),
            "seq",
            split_axis=0,
            concat_axis=0,
            tiled=True,
        ),
    )
    arrived_length = lax.all_to_all(
        send_length.reshape(seq_count, pair_limit), "seq", split_axis=0, concat_axis=0, tiled=True
    )
    slot_query = arrived_query.reshape(slot_count, query_pairs, row_width)
    slot_rows = arrived_rows.reshape(slot_count, 2, row_width)
    slot_length = arrived_length.reshape(slot_count)
    queries = slot_query.reshape(slot_count * query_pairs, row_width)
    start_state = empty_state((queries.shape[0],), lat_width)
    shard_rows = lax.all_gather(local_rows[0], "seq", axis=0, tiled=True)
    is_past, past_index, group_index = row_kinds(shard_rows.shape[0])
    allowed = jnp.where(is_past, past_index < past_len[0], True)[None, :]
    scores = (
        jnp.einsum("qc,kc->qk", queries, shard_rows, preferred_element_type=jnp.float32) * scale
    )
    result_state = merge_state(start_state, block_state(scores, allowed, shard_rows[:, :lat_width]))
    prefix_state = (
        result_state[0].reshape(slot_count, query_pairs),
        result_state[1].reshape(slot_count, query_pairs),
        result_state[2].reshape(slot_count, query_pairs, lat_width),
    )
    cache_scores = (
        jnp.einsum("nqc,nkc->nqk", slot_query, decode_pool, preferred_element_type=jnp.float32)
        * scale
    )
    cache_allowed = (
        jnp.arange(cache_length, dtype=jnp.int32)[None, None, :] < slot_length[:, None, None]
    )
    cache_state = block_state(cache_scores, cache_allowed, decode_pool[:, :, :lat_width])
    fresh_scores = (
        jnp.einsum("nqc,nkc->nqk", slot_query, slot_rows, preferred_element_type=jnp.float32)
        * scale
    )
    query_step = jnp.arange(query_pairs, dtype=jnp.int32) // head_local
    fresh_allowed = step_pair[None, None, :] <= query_step[None, :, None]
    fresh_state = block_state(fresh_scores, fresh_allowed, slot_rows[:, :, :lat_width])
    final_state = merge_state(merge_state(prefix_state, cache_state), fresh_state)
    latent_out = (
        (final_state[2] / final_state[1][..., None])
        .astype(jnp.bfloat16)
        .reshape(slot_count, 2, head_local, lat_width)
    )
    slot_out = jnp.einsum(
        "nshc,hcv->nshv", latent_out, w_value, preferred_element_type=jnp.float32
    ).astype(jnp.bfloat16)
    returned = lax.all_to_all(
        slot_out.reshape(seq_count, pair_limit, -1), "seq", split_axis=0, concat_axis=0, tiled=True
    )
    decode_out = jnp.dot(
        dispatch_half.T, returned.reshape(slot_count, -1), preferred_element_type=jnp.float32
    ).astype(jnp.bfloat16)
    decode_out = decode_out.reshape(request_local, 2, head_local, value_width)
    return (prefill_out, decode_out)


def solution(mesh):
    in_specs = (
        P(None, "seq", ("tp", "grp")),
        P(None, "seq", ("tp", "grp"), None),
        P(None, "seq", None),
        P(),
        P("seq", None, ("tp", "grp")),
        P("seq", None, ("tp", "grp"), None),
        P("seq", None, None),
        P("seq", None),
        P("seq"),
        P(("tp", "grp"), None),
        P(),
        P(("tp", "grp"), None, None),
    )
    out_specs = (P(None, "seq", ("tp", "grp"), None), P("seq", None, ("tp", "grp"), None))
    return jax.shard_map(
        on_device, mesh=mesh, in_specs=in_specs, out_specs=out_specs, check_vma=False
    )
```

profile of v0, /device:TPU:1, one launch (start us, length us, event | category | flops | bytes accessed | tf_op | source)
XLA Modules:
  0.0 339.5 jit_solution(11042230814303577639)
XLA Ops:
  7.3 2.6 convolution_convert_fusion.3
  10.0 0.7 broadcast_add_fusion.1
  10.6 0.1 add_convert_fusion
  10.7 60.8 %all-reduce.2.cloned.1.call-done = bf16[4,32,576]{2,1,0:T(8,128)(2,1)} async-done(((bf16[4,32,576]{2,1,0:T(8,128)(2,1)}), bf16[4,32,576]{2,1,0:T(8,128)(2,1)}) %all-reduce.2.cloned.1.call-update) | async-done | bytes 147472 | tf_op jit(solution)/shard_map/psum | solution.py:98
  71.5 0.9 convert_element_type.86
  72.4 0.1 multiply_reduce_fusion
  72.5 0.3 fusion.66
  72.9 0.8 multiply_convert_fusion
  73.6 2.4 maximum_maximum_fusion
  76.0 1.7 slice.59
  77.8 0.7 all-gather.4.cloned.1.call-update
  78.5 0.2 convert_reduce_fusion
  78.7 0.1 select_reduce_fusion
  78.8 0.7 all_to_all.16
  79.4 6.7 %all-to-all-start.1 = ((s32[16,1,2]{2,1,0:T(1,128)}), s32[16,1,2]{2,1,0:T(1,128)S(1)}, u32[]{:S(2)}, u32[]{:S(2)}) async-start(s32[16,1,2]{2,1,0:T(1,128)} %bitcast.11), calls=%async_computation.1 | async-start | bytes 16384 | tf_op jit(solution)/shard_map/all_to_all | solution.py:175
  86.1 1.6 convolution_convert_fusion.4
  87.8 23.6 %psum.15 = bf16[16,2,576]{2,0,1:T(8,128)(2,1)S(1)} all-reduce(bf16[16,2,576]{2,0,1:T(8,128)(2,1)S(1)} %convolution_convert_fusion.4), channel_id=1, replica_groups=mesh['seq'=16,'tp'=4,'grp'=2] {'tp','grp'}, use_global_device_ids=true, to_apply=%region_8.9 | all-reduce | flops 18432 | bytes 73728 | tf_op jit(solution)/shard_map/psum | solution.py:99
  111.4 0.1 multiply_reduce_fusion.1
  111.5 0.1 fusion.86
  111.7 0.1 multiply_convert_fusion.1
  111.8 0.1 pad_maximum_fusion
  111.9 0.1 convert_element_type.100
  112.0 1.9 reshape.417
  114.0 0.3 convolution_convert_fusion.2
  114.3 1.6 convolution_convert_fusion
  115.9 0.7 reshape.421
  116.5 2.7 reshape.418
  119.2 6.2 %all-to-all-start.2 = ((bf16[16,2,1152]{2,1,0:T(2,128)(2,1)}), bf16[16,2,1152]{2,1,0:T(2,128)(2,1)S(1)}, u32[]{:S(2)}, u32[]{:S(2)}) async-start(bf16[16,2,1152]{2,1,0:T(2,128)(2,1)} %reshape.421), calls=%async_computation.2 | async-start | bytes 147456 | tf_op jit(solution)/shard_map/all_to_all | solution.py:167
  125.5 7.3 %all-to-all-done.2 = bf16[16,2,1152]{2,1,0:T(2,128)(2,1)S(1)} async-done(((bf16[16,2,1152]{2,1,0:T(2,128)(2,1)}), bf16[16,2,1152]{2,1,0:T(2,128)(2,1)S(1)}, u32[]{:S(2)}, u32[]{:S(2)}) %all-to-all-start.2) | async-done | bytes 73760 | tf_op jit(solution)/shard_map/all_to_all | solution.py:167
  132.7 4.6 %all-to-all-start = ((bf16[16,2,18432]{2,1,0:T(2,128)(2,1)}), bf16[16,2,18432]{2,1,0:T(2,128)(2,1)}, u32[]{:S(2)}, u32[]{:S(2)}) async-start(bf16[16,2,18432]{2,1,0:T(2,128)(2,1)} %reshape.418), calls=%async_computation | async-start | bytes 2359296 | tf_op jit(solution)/shard_map/all_to_all | solution.py:160
  137.3 2.6 broadcast_compare_fusion
  139.9 0.5 broadcast.420
  140.4 0.7 reduce.3
  141.1 0.1 lt.102
  141.1 0.1 iota_compare_fusion
  141.2 0.1 reshape.422
  141.4 10.0 %all-to-all-done = bf16[16,2,18432]{2,1,0:T(2,128)(2,1)} async-done(((bf16[16,2,18432]{2,1,0:T(2,128)(2,1)}), bf16[16,2,18432]{2,1,0:T(2,128)(2,1)}, u32[]{:S(2)}, u32[]{:S(2)}) %all-to-all-start) | async-done | bytes 1179680 | tf_op jit(solution)/shard_map/all_to_all | solution.py:160
  151.4 4.2 %reshape.420 = bf16[32,32,576]{2,1,0:T(8,128)(2,1)} reshape(bf16[16,2,18432]{2,1,0:T(2,128)(2,1)} %all-to-all-done) | data formatting | bytes 2359296 | tf_op jit(solution)/shard_map/reshape | solution.py:178
  155.6 4.2 %reshape_reshape.3 = bf16[1024,576]{1,0:T(8,128)(2,1)} reshape(bf16[16,2,18432]{2,1,0:T(2,128)(2,1)} %all-to-all-done) | data formatting | bytes 2359296 | tf_op jit(solution)/shard_map/reshape;reshape | solution.py:181
  159.8 1.9 fusion.124
  161.8 8.0 %fusion.123 = (f32[32,32]{1,0:T(8,128)S(1)}, f32[32,32,384]{2,1,0:T(8,128)S(1)}) fusion(bf16[32,32,576]{2,1,0:T(8,128)(2,1)} %reshape.420, bf16[32,384,576]{1,2,0:T(8,128)(2,1)} %param.18, pred[32,384]{1,0:T(8,128)(4,1)S(1)} %iota_compare_fusion), kind=kOutput, calls=%fused_computation.170 | convolution fusion | flops 454163456 | bytes 16924672 | tf_op jit(solution)/shard_map/nqc,nkc->nqk/dot_general | solution.py:196
  169.8 0.5 fusion.39
  170.3 9.9 %fusion.13 = f32[32,32,512]{2,1,0:T(8,128)} fusion(bf16[32,384,576]{1,2,0:T(8,128)(2,1)} %param.18, f32[32,32,384]{2,1,0:T(8,128)S(1)} %get-tuple-element.27, f32[32,32]{1,0:T(8,128)S(1)} %get-tuple-element.26, pred[32,384]{1,0:T(8,128)(4,1)S(1)} %iota_compare_fusion), kind=kOutput, calls=%fused_computation.17 | convolution fusion | flops 403832832 | bytes 16269312 | tf_op jit(solution)/shard_map/...qk,...kc->...qc/dot_general | solution.py:38
  180.2 12.7 %fusion.12 = (f32[1024]{0:T(1024)S(1)}, f32[1024,3584]{1,0:T(8,128)}) fusion(pred[3584]{0:T(1024)(128)(4,1)S(1)} %compare_select_fusion, bf16[1024,576]{1,0:T(8,128)(2,1)} %reshape_reshape.3, bf16[1,3584,576]{2,1,0:T(8,128)(2,1)} %all-gather.6.cloned.1.call-done), kind=kOutput, calls=%fused_computation.16 | convolution fusion | flops 4238867456 | bytes 19996160 | tf_op jit(solution)/shard_map/qc,kc->qk/dot_general | solution.py:187
  193.0 9.3 %fusion.15 = f32[1024]{0:T(1024)S(1)} fusion(f32[1024,3584]{1,0:T(8,128)} %get-tuple-element.29, f32[1024]{0:T(1024)S(1)} %get-tuple-element.28, pred[3584]{0:T(1024)(128)(4,1)S(1)} %compare_select_fusion), kind=kLoop, calls=%fused_computation.19 | loop fusion | flops 18349056 | bytes 14691840 | tf_op jit(solution)/shard_map/reduce_sum | solution.py:37
  202.3 0.1 reduce_sum.80
  202.4 9.1 %multiply_add_fusion = f32[1024,512]{1,0:T(8,128)S(1)} fusion(bf16[3584,576]{1,0:T(8,128)(2,1)} %bitcast.75, f32[1024,3584]{1,0:T(8,128)} %get-tuple-element.29, f32[1024]{0:T(1024)S(1)} %get-tuple-element.28, pred[3584]{0:T(1024)(128)(4,1)S(1)} %compare_select_fusion, f32[1024]{0:T(1024)S(1)} %get-tuple-element.23, f32[1024]{0:T(1024)S(1)} %get-tuple-element.22), kind=kOutput, calls=%fused_computation.34 | convolution fusion | flops 3777495040 | bytes 20463104 | tf_op jit(solution)/shard_map/...qk,...kc->...qc/dot_general | solution.py:38
  211.5 1.2 divide_convert_fusion.1
  212.7 0.5 copy-done.4
  213.2 1.3 fusion.49
  214.5 0.2 copy.48
  214.7 0.8 reshape.424
  215.5 4.4 %all-to-all-start.3 = ((bf16[16,2,4096]{2,1,0:T(2,128)(2,1)}), bf16[16,2,4096]{2,1,0:T(2,128)(2,1)S(1)}, u32[]{:S(2)}, u32[]{:S(2)}) async-start(bf16[16,2,4096]{2,1,0:T(2,128)(2,1)} %reshape.424), calls=%async_computation.3 | async-start | bytes 524288 | tf_op jit(solution)/shard_map/all_to_all | solution.py:219
  219.8 0.1 broadcast_compare_fusion.1
  220.0 10.2 %all-to-all-done.3 = bf16[16,2,4096]{2,1,0:T(2,128)(2,1)S(1)} async-done(((bf16[16,2,4096]{2,1,0:T(2,128)(2,1)}), bf16[16,2,4096]{2,1,0:T(2,128)(2,1)S(1)}, u32[]{:S(2)}, u32[]{:S(2)}) %all-to-all-start.3) | async-done | bytes 262176 | tf_op jit(solution)/shard_map/all_to_all | solution.py:219
  230.2 0.1 reshape.425
  230.3 0.2 fusion.52
  230.5 0.7 copy.54
  231.2 30.8 %all-gather.4.cloned.1.call-done = bf16[4,3584,576]{2,1,0:T(8,128)(2,1)} async-done(((bf16[4,224,576]{2,1,0:T(8,128)(2,1)}), bf16[4,3584,576]{2,1,0:T(8,128)(2,1)}) %all-gather.4.cloned.1.call-update) | async-done | bytes 16515088 | tf_op jit(solution)/shard_map/all_gather | solution.py:124
  262.0 23.4 %fusion = (f32[4,512]{1,0:T(4,128)S(1)}, f32[4,3584,512]{2,1,0:T(8,128)}) fusion(pred[512,3584]{0,1:T(8,128)(4,1)} %broadcast_compare_fusion, pred[4,3584]{1,0:T(4,128)(4,1)S(1)} %broadcast_compare_fusion.1, pred[3584]{0:T(1024)(128)(4,1)S(1)} %fusion.95, bf16[4,3584,576]{2,1,0:T(8,128)(2,1)} %all-gather.4.cloned.1.call-done, ...), kind=kOutput, calls=%fused_computation.2 | convolution fusion | flops 8485074944 | bytes 50095616 | tf_op jit(solution)/shard_map/pqc,pkc->pqk/dot_general | solution.py:132
  285.5 17.1 %fusion.1 = f32[4,512]{1,0:T(4,128)S(1)} fusion(f32[4,3584,512]{2,1,0:T(8,128)} %get-tuple-element.25, f32[4,512]{1,0:T(4,128)S(1)} %get-tuple-element.24, pred[512,3584]{0,1:T(8,128)(4,1)S(1)} %copy-done.2, pred[4,3584]{1,0:T(4,128)(4,1)S(1)} %broadcast_compare_fusion.1, pred[3584]{0:T(1024)(128)(4,1)S(1)} %fusion.95), kind=kLoop, calls=%fused_computation.4 | loop fusion | flops 44038144 | bytes 31229440 | tf_op jit(solution)/shard_map/reduce_sum | solution.py:37
  302.6 25.2 %divide_convert_fusion = bf16[4,512,512]{2,1,0:T(8,128)(2,1)} fusion(bf16[4,3584,576]{2,1,0:T(8,128)(2,1)S(1)} %copy-done.9, f32[4,3584,512]{2,1,0:T(8,128)} %get-tuple-element.25, f32[4,512]{1,0:T(4,128)S(1)} %get-tuple-element.24, pred[512,3584]{0,1:T(8,128)(4,1)S(1)} %copy-done.2, pred[4,3584]{1,0:T(4,128)(4,1)S(1)} %broadcast_compare_fusion.1, ...), kind=kOutput, calls=%fused_computation.24 | convolution fusion | flops 7564427264 | bytes 48023552 | tf_op jit(solution)/shard_map/...qk,...kc->...qc/dot_general | solution.py:38
  327.7 4.1 %fusion.41 = bf16[4,32,16,128]{3,1,0,2:T(8,128)(2,1)S(1)} fusion(bf16[16,512,128]{2,1,0:T(8,128)(2,1)S(1)} %copy-done.5, bf16[4,32,16,512]{3,2,1,0:T(8,128)(2,1)} %bitcast.78), kind=kOutput, calls=%fused_computation.40 | convolution fusion | flops 268697600 | bytes 4718592 | tf_op jit(solution)/shard_map/pthc,hcv->pthv/dot_general | solution.py:140
  331.8 1.1 copy.49
  (50 shorter events, 0.6 us)
Async XLA Ops:
  7.2 254.9 %copy-start = (bf16[4,32,16,576]{3,2,1,0:T(8,128)(2,1)S(1)}, bf16[4,32,16,576]{3,2,1,0:T(8,128)(2,1)}, u32[]{:S(2)}) copy-start(bf16[4,32,16,576]{3,2,1,0:T(8,128)(2,1)} %param.13) | copy-start | bytes 7077892
  7.2 104.2 %copy-start.8 = (s32[4]{0:T(128)S(1)}, s32[4]{0:T(128)}, u32[]{:S(2)}) copy-start(s32[4]{0:T(128)} %param.15) | copy-start | bytes 52
  7.2 104.5 %copy-start.7 = (f32[512]{0:T(512)S(1)}, f32[512]{0:T(512)}, u32[]{:S(2)}) copy-start(f32[512]{0:T(512)} %param.22) | copy-start | bytes 6148
  7.2 71.3 %copy-start.10 = (s32[16,1]{0,1:T(1,128)S(1)}, s32[16,1]{0,1:T(1,128)}, u32[]{:S(2)}) copy-start(s32[16,1]{0,1:T(1,128)} %param.19) | copy-start | bytes 196
  7.2 71.4 %copy-start.11 = (s32[16]{0:T(128)S(1)}, s32[16]{0:T(128)}, u32[]{:S(2)}) copy-start(s32[16]{0:T(128)} %param.20) | copy-start | bytes 196
  7.2 78.9 %copy-start.6 = (bf16[16,2,896]{2,1,0:T(2,128)(2,1)S(1)}, bf16[16,2,896]{2,1,0:T(2,128)(2,1)}, u32[]{:S(2)}) copy-start(bf16[16,2,896]{2,1,0:T(2,128)(2,1)} %param.16) | copy-start | bytes 172036
  7.2 64.2 %all-reduce.2.cloned.1.call-start = ((), (), s32[]{:S(2)}) async-start(), calls=%async_computation.4 | async-start | bytes 327680 | tf_op jit(solution)/shard_map/psum | solution.py:98
  9.9 170.3 %all-gather.6.cloned.1.call-start = ((), (), s32[]{:S(2)}) async-start(), calls=%async_computation.6 | async-start | bytes 4874240 | tf_op jit(solution)/shard_map/all_gather | solution.py:183
  77.7 184.3 %all-gather.4.cloned.1.call-start = ((), (), s32[]{:S(2)}) async-start(), calls=%async_computation.5 | async-start | bytes 19496960 | tf_op jit(solution)/shard_map/all_gather | solution.py:124
  79.4 39.8 %all-to-all-start.1 = ((s32[16,1,2]{2,1,0:T(1,128)}), s32[16,1,2]{2,1,0:T(1,128)S(1)}, u32[]{:S(2)}, u32[]{:S(2)}) async-start(s32[16,1,2]{2,1,0:T(1,128)} %bitcast.11), calls=%async_computation.1 | async-start | bytes 16384 | tf_op jit(solution)/shard_map/all_to_all | solution.py:175
  119.2 13.5 %all-to-all-start.2 = ((bf16[16,2,1152]{2,1,0:T(2,128)(2,1)}), bf16[16,2,1152]{2,1,0:T(2,128)(2,1)S(1)}, u32[]{:S(2)}, u32[]{:S(2)}) async-start(bf16[16,2,1152]{2,1,0:T(2,128)(2,1)} %reshape.421), calls=%async_computation.2 | async-start | bytes 147456 | tf_op jit(solution)/shard_map/all_to_all | solution.py:167
  132.7 18.6 %all-to-all-start = ((bf16[16,2,18432]{2,1,0:T(2,128)(2,1)}), bf16[16,2,18432]{2,1,0:T(2,128)(2,1)}, u32[]{:S(2)}, u32[]{:S(2)}) async-start(bf16[16,2,18432]{2,1,0:T(2,128)(2,1)} %reshape.418), calls=%async_computation | async-start | bytes 2359296 | tf_op jit(solution)/shard_map/all_to_all | solution.py:160
  202.4 9.1 %copy-start.3 = (f32[32,32,512]{2,1,0:T(8,128)S(1)}, f32[32,32,512]{2,1,0:T(8,128)}, u32[]{:S(2)}) copy-start(f32[32,32,512]{2,1,0:T(8,128)} %fusion.13) | copy-start | bytes 6291460
  211.5 1.7 copy-start.4
  215.5 14.7 %all-to-all-start.3 = ((bf16[16,2,4096]{2,1,0:T(2,128)(2,1)}), bf16[16,2,4096]{2,1,0:T(2,128)(2,1)S(1)}, u32[]{:S(2)}, u32[]{:S(2)}) async-start(bf16[16,2,4096]{2,1,0:T(2,128)(2,1)} %reshape.424), calls=%async_computation.3 | async-start | bytes 524288 | tf_op jit(solution)/shard_map/all_to_all | solution.py:219
  262.0 23.4 %copy-start.2 = (pred[512,3584]{0,1:T(8,128)(4,1)S(1)}, pred[512,3584]{0,1:T(8,128)(4,1)}, u32[]{:S(2)}) copy-start(pred[512,3584]{0,1:T(8,128)(4,1)} %broadcast_compare_fusion) | copy-start | bytes 5505028
  285.4 17.1 %copy-start.9 = (bf16[4,3584,576]{2,1,0:T(8,128)(2,1)S(1)}, bf16[4,3584,576]{2,1,0:T(8,128)(2,1)}, u32[]{:S(2)}) copy-start(bf16[4,3584,576]{2,1,0:T(8,128)(2,1)} %all-gather.4.cloned.1.call-done) | copy-start | bytes 49545220
  302.6 25.2 %copy-start.5 = (bf16[16,512,128]{2,1,0:T(8,128)(2,1)S(1)}, bf16[16,512,128]{2,1,0:T(8,128)(2,1)}, u32[]{:S(2)}) copy-start(bf16[16,512,128]{2,1,0:T(8,128)(2,1)} %param.23) | copy-start | bytes 6291460
  302.6 30.4 %copy-start.1 = (bf16[4,32,16,576]{3,2,1,0:T(8,128)(2,1)S(1)}, bf16[4,32,16,576]{3,2,1,0:T(8,128)(2,1)}, u32[]{:S(2)}) copy-start(bf16[4,32,16,576]{3,2,1,0:T(8,128)(2,1)} %param.13) | copy-start | bytes 7077892
Sparse Core Ops, SparseCore 0:
  11.0 60.4 all-reduce.1
  77.8 54.1 all-gather.5
  134.4 127.5 all-gather.3
where the time goes:
time: 340 us; the launch traced here: 339 us
  waiting for transfers between devices  120 us (35%)
  matrix products  103 us (30%)
  other arithmetic  36.5 us (11%)
  blocking collectives  23.6 us (7%)
  starting transfers between devices  21.9 us (6%)
  local copies, waits for them, and re-layouts  20.5 us (6%)
  between operations  14.2 us (4%)
    psum x1, waiting for transfers between devices, on_device(): lax.psum(group_latent.astype(jnp.bfloat16), ('tp', 'grp'))  60.8 us
    dot_general x4, matrix products, block_state(): jnp.einsum('...qk,...kc->...qc', weights.astype(jnp.bfloat16), values, pr...  45.4 us
    all_gather x1, waiting for transfers between devices, on_device(): shard_rows = lax.all_gather(local_rows, 'seq', axis=1, tiled=True)  30.8 us
    reduce_sum x4, other arithmetic, block_state(): totals = jnp.sum(weights, axis=-1)  27 us
    psum x1, blocking collectives, on_device(): lax.psum(decode_latent.astype(jnp.bfloat16), ('tp', 'grp'))  23.6 us
    dot_general x1, matrix products, on_device(): jnp.einsum('pqc,pkc->pqk', group_flat, shard_rows, preferred_element_type...  23.4 us
    dot_general x1, matrix products, on_device(): jnp.einsum('qc,kc->qk', queries, shard_rows, preferred_element_type=jnp.f...  12.7 us
    all_to_all x1, waiting for transfers between devices, on_device(): lax.all_to_all(slot_out.reshape(seq_count, pair_limit, -1), 'seq', split_...  10.2 us
  transfers between devices with their start and end apart: 7, of which 5 were waited for; matrix products, arithmetic and copies ran while one was open for 23% of the time, Pallas kernels for 0%

commit v1 on v0

v1 whole, which is shorter than its diff:
```python
import functools

import jax
import jax.numpy as jnp
from jax import lax
from jax.experimental import pallas as pl
from jax.experimental.pallas import tpu as pltpu
from jax.sharding import PartitionSpec as P

epsilon = 1e-06
negative = -1e30
log2_e = 1.4426950408889634
NT = (((1,), (1,)), ((), ()))
NN = (((1,), (0,)), ((), ()))
VMEM_BYTES = 56 * 2**20


def rotate(rope_part, positions):
    half_width = rope_part.shape[-1] // 2
    frequency = jnp.exp(-jnp.log(10000.0) * jnp.arange(half_width).astype(jnp.float32) / half_width)
    angles = positions.astype(jnp.float32)[..., None] * frequency
    cosine = jnp.cos(angles)
    sine_part = jnp.sin(angles)
    former = rope_part[..., :half_width]
    latter = rope_part[..., half_width:]
    return jnp.concatenate(
        [former * cosine - latter * sine_part, latter * cosine + former * sine_part], axis=-1
    )


def make_rows(latent, kv_gain, positions):
    lat_width = kv_gain.shape[0]
    latent_part = latent[..., :lat_width]
    spread = jnp.mean(latent_part * latent_part, axis=-1, keepdims=True)
    normed = latent_part * lax.rsqrt(spread + epsilon) * kv_gain
    return jnp.concatenate([normed, rotate(latent[..., lat_width:], positions)], axis=-1).astype(
        jnp.bfloat16
    )


def dot(left, right, dims):
    return lax.dot_general(left, right, dims, preferred_element_type=jnp.float32)


def key_scores(queries, keys, lat, dims):
    if dims is NT:
        return dot(queries[:, :lat], keys[:, :lat], NT) + dot(queries[:, lat:], keys[:, lat:], NT)
    return dot(queries[:, :lat], keys[:lat], NN) + dot(queries[:, lat:], keys[lat:], NN)


def lane_fold(op, total, block):
    for start in range(0, block.shape[1], 128):
        part = block[:, start : start + 128]
        total = part if total is None else op(total, part)
    return total


def attend_body(shape, info, q_ref, past_ref, group_ref, token_ref, *rest):
    tile, lat, factor, head_local, decode, chunk = shape
    if decode:
        fresh_ref, out_ref, lse_ref, hold = rest
    else:
        out_ref, hold = rest
    rows = q_ref.shape[0]
    pieces, piece_rows, width = past_ref.shape
    step = chunk // piece_rows
    past_count = pieces // step
    past_total = pieces * piece_rows
    half_past = past_total // 2
    past_len = info[0] if decode else info[pl.program_id(0)]

    def past_keys(j):
        return past_ref[j * step : (j + 1) * step].reshape(chunk, width)

    def group_keys():
        return group_ref[...].reshape(group_ref.shape[0] * group_ref.shape[1], width)

    group_total = group_ref.shape[0] * group_ref.shape[1]
    for i in range(rows // tile):
        span = pl.ds(i * tile, tile)
        queries = q_ref[span, :]
        row = lax.broadcasted_iota(jnp.int32, (tile, 1), 0) + i * tile
        highest = None
        for j in range(past_count):
            scores = key_scores(queries, past_keys(j), lat, NT)
            if (j + 1) * chunk > half_past:
                place = lax.broadcasted_iota(jnp.int32, (1, chunk), 1) + j * chunk
                scores = jnp.where(place < past_len, scores, negative)
            hold[i % 2, :, j * chunk : (j + 1) * chunk] = scores
            highest = lane_fold(jnp.maximum, highest, scores)
        scores = key_scores(queries, group_keys(), lat, NT)
        if not decode:
            token = info[4] + row // head_local
            scores = jnp.where(token_ref[...] <= token, scores, negative)
        hold[i % 2, :, past_total : past_total + group_total] = scores
        highest = lane_fold(jnp.maximum, highest, scores)
        if decode:
            fresh = fresh_ref[...]
            scores = key_scores(queries, fresh, lat, NT)
            place = lax.broadcasted_iota(jnp.int32, (1, fresh.shape[0]), 1)
            request = row // (2 * head_local)
            last = row // head_local
            scores = jnp.where((place >= 2 * request) & (place <= last), scores, negative)
            fresh_span = slice(past_total + group_total, past_total + group_total + fresh.shape[0])
            hold[i % 2, :, fresh_span] = scores
            highest = lane_fold(jnp.maximum, highest, scores)
        peak = jnp.max(highest, axis=1, keepdims=True)
        total = None
        summed = None
        parts = [
            (slice(j * chunk, (j + 1) * chunk), functools.partial(past_keys, j))
            for j in range(past_count)
        ]
        parts.append((slice(past_total, past_total + group_total), group_keys))
        if decode:
            parts.append((fresh_span, lambda: fresh_ref[...]))
        for place, keys in parts:
            weights = jnp.exp2((hold[i % 2, :, place] - peak) * factor)
            total = lane_fold(jnp.add, total, weights)
            part = dot(weights.astype(jnp.bfloat16), keys()[:, :lat], NN)
            summed = part if summed is None else summed + part
        total = jnp.sum(total, axis=1, keepdims=True)
        out_ref[span, :] = (summed / total).astype(jnp.bfloat16)
        if decode:
            lse = peak * factor + jnp.log2(total)
            lse_ref[span, :] = jnp.broadcast_to(lse, (tile, lse_ref.shape[1]))


def attend(info, query, past, group, token, fresh, lat, factor, head_local):
    decode = fresh is not None
    count, rows, width = query.shape
    pieces, _, piece_rows, _ = past.shape
    group_pieces, _, group_rows, _ = group.shape
    keys = pieces * piece_rows + group_pieces * group_rows
    tile = min(256, rows)
    chunk = 768
    in_specs = [
        pl.BlockSpec((None, rows, width), lambda p, _: (p, 0, 0)),
        pl.BlockSpec((pieces, None, piece_rows, width), lambda p, _: (0, p, 0, 0)),
        pl.BlockSpec((group_pieces, None, group_rows, width), lambda p, _: (0, p, 0, 0)),
        pl.BlockSpec(token.shape, lambda p, _: (0, 0)),
    ]
    operands = [query, past, group, token]
    out_specs = [pl.BlockSpec((None, rows, lat), lambda p, _: (p, 0, 0))]
    out_shape = [jax.ShapeDtypeStruct((count, rows, lat), jnp.bfloat16)]
    if decode:
        in_specs.append(pl.BlockSpec(fresh.shape, lambda p, _: (0, 0)))
        operands.append(fresh)
        keys += fresh.shape[0]
        out_specs.append(pl.BlockSpec((None, rows, 128), lambda p, _: (p, 0, 0)))
        out_shape.append(jax.ShapeDtypeStruct((count, rows, 128), jnp.float32))
    shape = (tile, lat, factor, head_local, decode, chunk)
    return pl.pallas_call(
        functools.partial(attend_body, shape),
        grid_spec=pltpu.PrefetchScalarGridSpec(
            num_scalar_prefetch=1,
            grid=(count,),
            in_specs=in_specs,
            out_specs=out_specs,
            scratch_shapes=[pltpu.VMEM((2, tile, keys), jnp.float32)],
        ),
        out_shape=out_shape,
        compiler_params=pltpu.CompilerParams(vmem_limit_bytes=VMEM_BYTES),
        cost_estimate=pl.CostEstimate(
            flops=2 * count * rows * keys * (768 + lat),
            bytes_accessed=2 * count * (keys + 2 * rows) * width,
            transcendentals=count * rows * keys,
        ),
        name="attend_decode" if decode else "attend_prefill",
    )(info, *operands)


def dispatch_body(source, length, q_ref, out_ref):
    slots, rows, width = out_ref.shape
    lat_rope = q_ref.shape[2]
    lane = lax.broadcasted_iota(jnp.int32, (rows, width - lat_rope), 1)
    for slot in range(slots):
        out_ref[slot, :, :lat_rope] = q_ref[source[slot]]
        size = length[slot]
        tail = jnp.where(lane < 32, size // 16, size % 16)
        out_ref[slot, :, lat_rope:] = tail.astype(jnp.float32).astype(jnp.bfloat16)


def dispatch_queries(source, length, query, width):
    slots = source.shape[0]
    _, rows, _ = query.shape
    smem = pl.BlockSpec(memory_space=pltpu.SMEM)
    vmem = pl.BlockSpec(memory_space=pltpu.VMEM)
    return pl.pallas_call(
        dispatch_body,
        in_specs=[smem, smem, vmem],
        out_specs=vmem,
        out_shape=jax.ShapeDtypeStruct((slots, rows, width), jnp.bfloat16),
        compiler_params=pltpu.CompilerParams(vmem_limit_bytes=VMEM_BYTES),
        name="dispatch_queries",
    )(source, length, query)


def cache_body(lat, factor, batch, order, length, used, q_ref, *rest):
    pool_refs = rest[:batch]
    out_ref, lse_ref = rest[batch:]
    step = pl.program_id(0)
    rows = q_ref.shape[1]
    width, cache_rows = pool_refs[0].shape

    @pl.when(step * batch < used[0])
    def _():
        place = lax.broadcasted_iota(jnp.int32, (1, cache_rows), 1)
        lane = lax.broadcasted_iota(jnp.int32, (rows, lse_ref.shape[2]), 1)
        slots = [order[step * batch + b] for b in range(batch)]
        scores = [
            key_scores(q_ref[slots[b], :, :width], pool_refs[b][...], lat, NN)
            for b in range(batch)
        ]
        for b in range(batch):
            masked = jnp.where(place < length[slots[b]], scores[b], negative)
            peak = jnp.max(masked, axis=1, keepdims=True)
            weights = jnp.exp2((masked - peak) * factor)
            total = jnp.sum(weights, axis=1, keepdims=True)
            summed = dot(weights.astype(jnp.bfloat16), pool_refs[b][:lat], NT)
            out_ref[slots[b]] = (summed / total).astype(jnp.bfloat16)
            lse = peak * factor + jnp.log2(total)
            high = lse.astype(jnp.bfloat16).astype(jnp.float32)
            middle = (lse - high).astype(jnp.bfloat16).astype(jnp.float32)
            low = lse - high - middle
            lse_ref[slots[b]] = jnp.where(
                lane == 0, high, jnp.where(lane == 1, middle, low)
            ).astype(jnp.bfloat16)


def attend_cache(order, length, used, query, pool, lat, factor):
    batch = 4
    slots, rows, padded = query.shape
    _, width, cache_rows = pool.shape
    whole = pl.BlockSpec((slots, rows, padded), lambda i, *_: (0, 0, 0))

    def pool_spec(b):
        return pl.BlockSpec(
            (None, width, cache_rows), lambda i, order, *_: (order[i * batch + b], 0, 0)
        )

    return pl.pallas_call(
        functools.partial(cache_body, lat, factor, batch),
        grid_spec=pltpu.PrefetchScalarGridSpec(
            num_scalar_prefetch=3,
            grid=(slots // batch,),
            in_specs=[whole] + [pool_spec(b) for b in range(batch)],
            out_specs=[
                pl.BlockSpec((slots, rows, lat), lambda i, *_: (0, 0, 0)),
                pl.BlockSpec((slots, rows, 128), lambda i, *_: (0, 0, 0)),
            ],
        ),
        out_shape=[
            jax.ShapeDtypeStruct((slots, rows, lat), jnp.bfloat16),
            jax.ShapeDtypeStruct((slots, rows, 128), jnp.bfloat16),
        ],
        compiler_params=pltpu.CompilerParams(vmem_limit_bytes=VMEM_BYTES),
        cost_estimate=pl.CostEstimate(
            flops=2 * slots * 128 * cache_rows * (width + lat),
            bytes_accessed=2 * slots * cache_rows * width,
            transcendentals=slots * rows * cache_rows,
        ),
        name="attend_cache",
    )(order, length, used, query, *([pool] * batch))


def merge_body(slot, back_ref, near_ref, near_lse_ref, out_ref):
    count = near_ref.shape[0]
    width = near_ref.shape[2]
    for r in range(count):
        back = back_ref[slot[r]].astype(jnp.float32)
        far = back[:, :width]
        far_lse = back[:, width : width + 1] + back[:, width + 1 : width + 2]
        far_lse = far_lse + back[:, width + 2 : width + 3]
        near_lse = near_lse_ref[r][:, :1]
        peak = jnp.maximum(far_lse, near_lse)
        far_part = jnp.exp2(far_lse - peak)
        near_part = jnp.exp2(near_lse - peak)
        mixed = far * far_part + near_ref[r] * near_part
        out_ref[r] = (mixed / (far_part + near_part)).astype(jnp.bfloat16)


def merge_decode(slot, back, near, near_lse):
    smem = pl.BlockSpec(memory_space=pltpu.SMEM)
    vmem = pl.BlockSpec(memory_space=pltpu.VMEM)
    return pl.pallas_call(
        merge_body,
        in_specs=[smem, vmem, vmem, vmem],
        out_specs=vmem,
        out_shape=jax.ShapeDtypeStruct(near.shape, jnp.bfloat16),
        compiler_params=pltpu.CompilerParams(vmem_limit_bytes=VMEM_BYTES),
        name="merge_decode",
    )(slot, back, near, near_lse)


def swap_core(value):
    return lax.ppermute(value, "grp", [(0, 1), (1, 0)])


def fetch_tp(value, shift):
    return lax.ppermute(value, "tp", [((i + shift) % 4, i) for i in range(4)])


def fetch_x(value, shift):
    return lax.ppermute(
        value, "seq", [(i // 4 * 4 + (i + shift) % 4, i) for i in range(16)]
    )


def fetch_z(value, shift):
    return lax.ppermute(value, "seq", [((i + 4 * shift) % 16, i) for i in range(16)])


def on_device(
    group_hidden,
    group_query,
    past_cache,
    past_len,
    decode_hidden,
    decode_query,
    decode_pool,
    owner,
    dec_len,
    w_latent,
    kv_gain,
    w_value,
):
    seq_count = lax.axis_size("seq")
    seq_place = lax.axis_index("seq")
    tp_place = lax.axis_index("tp")
    core = lax.axis_index("grp")
    z_place, x_place = seq_place // 4, seq_place % 4
    prompt_count, group_local, head_local, row_width = group_query.shape
    past_local = past_cache.shape[1]
    request_local = decode_query.shape[0]
    lat = kv_gain.shape[0]
    value_width = w_value.shape[2]
    slot_count = decode_pool.shape[0]
    pair_limit = slot_count // seq_count
    query_pairs = 2 * head_local
    factor = (value_width + row_width - lat) ** (-0.5) * log2_e

    half = past_local // 2
    past_half = lax.dynamic_slice_in_dim(past_cache, core * half, half, axis=1)
    past_all = lax.all_gather(past_half, ("seq", "grp"), axis=0, tiled=False)

    targets = owner[:, 0]
    request_order = jnp.arange(request_local, dtype=jnp.int32)
    earlier = (targets[:, None] == targets[None, :]) & (
        request_order[None, :] < request_order[:, None]
    )
    slot_rank = jnp.sum(earlier.astype(jnp.int32), axis=1)
    destination = targets * pair_limit + slot_rank
    matches = jnp.arange(slot_count, dtype=jnp.int32)[:, None] == destination[None, :]
    source = jnp.sum(jnp.where(matches, request_order[None, :], 0), axis=1)
    send_length = jnp.sum(jnp.where(matches, dec_len[None, :], 0), axis=1)
    send_query = dispatch_queries(
        source,
        send_length,
        decode_query.reshape(request_local, query_pairs, row_width),
        row_width + 64,
    )
    arrived = lax.all_to_all(
        send_query.reshape(seq_count, pair_limit * query_pairs, row_width + 64),
        "seq",
        split_axis=0,
        concat_axis=0,
        tiled=True,
    ).reshape(slot_count, query_pairs, row_width + 64)
    marks = arrived[:, 0, row_width:].astype(jnp.float32)
    slot_length = (marks[:, 0] * 16 + marks[:, 32]).astype(jnp.int32)

    part_tokens = group_local // 8
    part_pairs = 2 * request_local // 8
    part_rows = prompt_count * part_tokens + part_pairs
    hidden_group = group_hidden.reshape(prompt_count, 8, part_tokens, -1).transpose(1, 0, 2, 3)
    hidden_decode = decode_hidden.reshape(8, part_pairs, -1)
    hidden = jnp.concatenate(
        [hidden_group.reshape(8, prompt_count * part_tokens, -1), hidden_decode], axis=1
    )
    partial = jnp.einsum("krd,dc->krc", hidden, w_latent, preferred_element_type=jnp.float32)
    partial = partial.astype(jnp.bfloat16).reshape(4, 2, part_rows, row_width)
    keep = lax.dynamic_index_in_dim(partial, core, axis=1, keepdims=False)
    give = lax.dynamic_index_in_dim(partial, 1 - core, axis=1, keepdims=False)
    pair_sum = (keep.astype(jnp.float32) + swap_core(give).astype(jnp.float32)).astype(jnp.bfloat16)
    latent = lax.dynamic_index_in_dim(pair_sum, tp_place, axis=0, keepdims=False)
    latent = latent.astype(jnp.float32)
    for shift in range(1, 4):
        sent = lax.dynamic_index_in_dim(
            pair_sum, (tp_place - shift) % 4, axis=0, keepdims=False
        )
        latent = latent + fetch_tp(sent, shift).astype(jnp.float32)
    part = tp_place * 2 + core
    token = part * part_tokens + jnp.arange(part_tokens, dtype=jnp.int32)
    group_positions = past_len[:, None] + seq_place * group_local + token[None, :]
    pair_index = part * part_pairs + jnp.arange(part_pairs, dtype=jnp.int32)
    decode_positions = (
        past_len[0] + group_local * seq_count + dec_len[pair_index // 2] + pair_index % 2
    )
    positions = jnp.concatenate([group_positions.reshape(-1), decode_positions])
    rows_own = make_rows(latent, kv_gain, positions)
    rows_tp = [rows_own] + [fetch_tp(rows_own, shift) for shift in range(1, 4)]
    tp_order = (tp_place + jnp.arange(4, dtype=jnp.int32)) % 4
    rows_tp = jnp.stack(rows_tp)

    fresh_own = rows_tp[:, prompt_count * part_tokens :]
    fresh_other = swap_core(fresh_own)
    fresh_even = jnp.where(core == 0, fresh_own, fresh_other)
    fresh_odd = jnp.where(core == 0, fresh_other, fresh_own)
    fresh = jnp.stack([fresh_even, fresh_odd], axis=1)
    fresh = fresh[(jnp.arange(4, dtype=jnp.int32) - tp_place) % 4]
    fresh = fresh.reshape(2 * request_local, row_width)
    fresh = jnp.pad(fresh, ((0, 128 - 2 * request_local), (0, 0)))

    group_own = rows_tp[:, : prompt_count * part_tokens].reshape(
        4, prompt_count, part_tokens, row_width
    )
    group_own = group_own.transpose(1, 0, 2, 3).reshape(prompt_count, 4 * part_tokens, row_width)
    group_x = jnp.stack([group_own] + [fetch_x(group_own, shift) for shift in range(1, 4)])
    group_z = jnp.stack([group_x] + [fetch_z(group_x, shift) for shift in range(1, 4)])
    group_z = group_z.reshape(16, prompt_count, 4 * part_tokens, row_width)
    group_all = jnp.concatenate([group_z, swap_core(group_z)], axis=0)
    ring = jnp.arange(4, dtype=jnp.int32)
    holder = ((z_place + ring) % 4)[:, None] * 4 + ((x_place + ring) % 4)[None, :]
    cores = jnp.stack([core, 1 - core])
    key_token = (
        holder.reshape(1, 16, 1, 1) * group_local
        + (tp_order.reshape(1, 1, 4, 1) * 2 + cores.reshape(2, 1, 1, 1)) * part_tokens
        + jnp.arange(part_tokens, dtype=jnp.int32).reshape(1, 1, 1, part_tokens)
    ).reshape(1, seq_count * group_local)

    is_used = slot_length > 0
    used_rank = jnp.cumsum(is_used.astype(jnp.int32)) - 1
    used = jnp.sum(is_used.astype(jnp.int32))
    slots = jnp.arange(slot_count, dtype=jnp.int32)
    wanted = jnp.minimum(slots, jnp.maximum(used - 1, 0))
    order = jnp.sum(
        jnp.where(is_used[None, :] & (used_rank[None, :] == wanted[:, None]), slots[None, :], 0),
        axis=1,
    )
    cache_latent, cache_lse = attend_cache(
        order, slot_length, used.reshape(1), arrived, jnp.swapaxes(decode_pool, 1, 2), lat, factor
    )
    cache_value = jnp.einsum(
        "nshc,hcv->nshv",
        cache_latent.reshape(slot_count, 2, head_local, lat),
        w_value,
        preferred_element_type=jnp.float32,
    ).astype(jnp.bfloat16)
    back = jnp.concatenate(
        [cache_value.reshape(slot_count, query_pairs, value_width), cache_lse], axis=-1
    )
    back = lax.all_to_all(
        back.reshape(seq_count, pair_limit * query_pairs, 2 * value_width),
        "seq",
        split_axis=0,
        concat_axis=0,
        tiled=True,
    ).reshape(slot_count, query_pairs, 2 * value_width)

    info = jnp.concatenate([past_len, (seq_place * group_local)[None]]).astype(jnp.int32)
    near_latent, near_lse = attend(
        info,
        decode_query.reshape(1, request_local * query_pairs, row_width),
        past_all,
        group_all,
        key_token,
        fresh,
        lat,
        factor,
        head_local,
    )
    near = jnp.einsum(
        "rshc,hcv->rshv",
        near_latent.reshape(request_local, 2, head_local, lat),
        w_value,
        preferred_element_type=jnp.float32,
    )
    decode_out = merge_decode(
        destination,
        back,
        near.reshape(request_local, query_pairs, value_width),
        near_lse.reshape(request_local, query_pairs, 128),
    ).reshape(request_local, 2, head_local, value_width)

    (prefill_latent,) = attend(
        info,
        group_query.reshape(prompt_count, group_local * head_local, row_width),
        past_all,
        group_all,
        key_token,
        None,
        lat,
        factor,
        head_local,
    )
    prefill_out = jnp.einsum(
        "pthc,hcv->pthv",
        prefill_latent.reshape(prompt_count, group_local, head_local, lat),
        w_value,
        preferred_element_type=jnp.float32,
    ).astype(jnp.bfloat16)
    return (prefill_out, decode_out)


def solution(mesh):
    in_specs = (
        P(None, "seq", ("tp", "grp")),
        P(None, "seq", ("tp", "grp"), None),
        P(None, "seq", None),
        P(),
        P("seq", None, ("tp", "grp")),
        P("seq", None, ("tp", "grp"), None),
        P("seq", None, None),
        P("seq", None),
        P("seq"),
        P(("tp", "grp"), None),
        P(),
        P(("tp", "grp"), None, None),
    )
    out_specs = (P(None, "seq", ("tp", "grp"), None), P("seq", None, ("tp", "grp"), None))
    return jax.shard_map(
        on_device, mesh=mesh, in_specs=in_specs, out_specs=out_specs, check_vma=False
    )
```

time: 340 us -> 183 us (0.54)
  matrix products: 103 us -> 8.67 us
  waiting for transfers between devices: 120 us -> 29.8 us
  Pallas kernels: 0 us -> 56.9 us
  blocking collectives: 23.6 us -> 0 us
  other arithmetic: 36.5 us -> 20.2 us
  starting transfers between devices: 21.9 us -> 35.9 us
  local copies, waits for them, and re-layouts: 20.5 us -> 15.4 us
    dot_general x15 -> x4, matrix products: 103 us -> 8.67 us  [the longest x1 2.58 us: on_device(): jnp.einsum('nshc,hcv->nshv', cache_latent.reshape(slot_count, 2, head_loc...]
    psum x1 -> x0, waiting for transfers between devices: 60.8 us -> none  [on_device(): lax.psum(group_latent.astype(jnp.bfloat16), ('tp', 'grp'))]
    pallas_call x0 -> x5, Pallas kernels: none -> 56.9 us  [the longest x2 37.9 us: attend(): pl.pallas_call(functools.partial(attend_body, shape), grid_spec=pltpu.Pre...]
    all_gather x2 -> x1, waiting for transfers between devices: 30.8 us -> 0.01 us  [on_device(): past_all = lax.all_gather(past_half, ('seq', 'grp'), axis=0, tiled=False)]
    ppermute x0 -> x15, waiting for transfers between devices: none -> 29.8 us  [the longest x3 24.5 us: fetch_z(): lax.ppermute(value, 'seq', [((i + 4 * shift) % 16, i) for i in range(16)])]
    all_to_all x4 -> x2, waiting for transfers between devices: 27.5 us -> 0.01 us  [the longest x1 0.01 us: on_device(): lax.all_to_all(send_query.reshape(seq_count, pair_limit * query_pairs, ro...]
    reduce_sum x5 -> x3, other arithmetic: 27 us -> 2.06 us  [the longest x1 0.72 us: on_device(): jnp.sum(jnp.where(is_used[None, :] & (used_rank[None, :] == wanted[:, Non...]
    psum x1 -> x0, blocking collectives: 23.6 us -> none  [on_device(): lax.psum(decode_latent.astype(jnp.bfloat16), ('tp', 'grp'))]
  transfers between devices with their start and end apart: 7 -> 18, of which waited for: 5 -> 8; matrix products, arithmetic and copies ran while one was open for 23% -> 22% of each run, Pallas kernels for 0% -> 30%
where the time goes in v1:
time: 183 us; the launch traced here: 182 us
  Pallas kernels  56.9 us (31%)
  starting transfers between devices  35.9 us (20%)
  waiting for transfers between devices  29.8 us (16%)
  other arithmetic  20.2 us (11%)
  local copies, waits for them, and re-layouts  15.4 us (8%)
  between operations  15.1 us (8%)
  matrix products  8.67 us (5%)
    pallas_call x2, Pallas kernels, attend(): pl.pallas_call(functools.partial(attend_body, shape), grid_spec=pltpu.Pre...  37.9 us
    ppermute x3, waiting for transfers between devices, fetch_z(): lax.ppermute(value, 'seq', [((i + 4 * shift) % 16, i) for i in range(16)])  24.5 us
    pallas_call x1, Pallas kernels, attend_cache(): pl.pallas_call(functools.partial(cache_body, lat, factor, batch), grid_sp...  13.6 us
    ppermute x3, starting transfers between devices, swap_core(): return lax.ppermute(value, 'grp', [(0, 1), (1, 0)])  10.1 us
    all_to_all x1, starting transfers between devices, on_device(): lax.all_to_all(send_query.reshape(seq_count, pair_limit * query_pairs, ro...  7.81 us
    ppermute x6, starting transfers between devices, fetch_tp(): return lax.ppermute(value, 'tp', [((i + shift) % 4, i) for i in range(4)])  6.04 us
    ppermute x6, waiting for transfers between devices, fetch_tp(): return lax.ppermute(value, 'tp', [((i + shift) % 4, i) for i in range(4)])  5.34 us
    all_to_all x1, starting transfers between devices, on_device(): lax.all_to_all(back.reshape(seq_count, pair_limit * query_pairs, 2 * valu...  4.6 us
  transfers between devices with their start and end apart: 18, of which 8 were waited for; matrix products, arithmetic and copies ran while one was open for 22% of the time, Pallas kernels for 30%

profile of v1, /device:TPU:1, one launch (start us, length us, event | category | flops | bytes accessed | tf_op | source)
XLA Modules:
  0.0 182.0 jit_solution(2580095088724042156)
XLA Ops:
  7.2 2.0 %constant_dynamic-slice_fusion = bf16[4,96,576]{2,1,0:T(8,128)(2,1)} fusion(bf16[4,192,576]{2,1,0:T(8,128)(2,1)} %param.14, s32[]{:T(128)S(6)} %select_n.144), kind=kLoop, calls=%fused_computation.91 | loop fusion | bytes 884740 | tf_op jit(solution)/shard_map/dynamic_slice | solution.py:344
  9.3 1.0 reshape.463
  10.5 1.8 convolution_convert_fusion
  12.3 0.7 copy-done.7
  13.0 1.5 collective-permute-start
  14.7 0.6 copy-done.12
  15.3 0.7 select_reduce_fusion.1
  16.0 2.5 %dispatch_queries.1 = bf16[32,32,640]{2,1,0:T(8,128)(2,1)} custom-call(s32[32]{0:T(128)} %get-tuple-element.19.source, s32[32]{0:T(128)} %get-tuple-element.18.length, bf16[16,32,576]{2,1,0:T(8,128)(2,1)} %bitcast.107), custom_call_target="tpu_custom_call" | custom-call | tf_op jit(solution)/shard_map/dispatch_queries/pallas_call | solution.py:189
  18.4 7.8 %all-to-all-start = ((bf16[16,64,640]{2,1,0:T(8,128)(2,1)}), bf16[16,64,640]{2,1,0:T(8,128)(2,1)S(1)}, u32[]{:S(2)}, u32[]{:S(2)}) async-start(bf16[16,64,640]{2,1,0:T(8,128)(2,1)} %bitcast.106), calls=%async_computation | async-start | bytes 2621440 | tf_op jit(solution)/shard_map/all_to_all | solution.py:363
  26.5 0.6 gather_fusion
  27.4 0.6 multiply_exponential_fusion
  28.1 0.6 pad_clamp_fusion
  28.9 0.7 iota_add_fusion
  29.6 0.6 pad_add_fusion.info
  30.2 1.0 fusion.32
  31.2 0.7 dynamic-slice_bitcast_fusion.3
  31.9 2.7 %collective-permute-start.1 = (bf16[20,576]{1,0:T(8,128)(2,1)}, bf16[20,576]{1,0:T(8,128)(2,1)}, u32[]{:S(2)}, u32[]{:S(2)}) collective-permute-start(bf16[20,576]{1,0:T(8,128)(2,1)} %get-tuple-element.22), channel_id=1, source_target_pairs={{2,0},{4,2},{6,4},{0,6},{3,1},{5,3},{7,5},{1,7},{10,8},{12,10},{14... | collective-permute-start | bytes 69128 | tf_op jit(solution)/shard_map/ppermute | solution.py:301
  34.9 0.7 collective-permute-start.3
  35.7 1.5 add.395.token_ref
  37.3 2.1 %collective-permute-done.2 = bf16[20,576]{1,0:T(8,128)(2,1)} collective-permute-done((bf16[20,576]{1,0:T(8,128)(2,1)}, bf16[20,576]{1,0:T(8,128)(2,1)}, u32[]{:S(2)}, u32[]{:S(2)}) %collective-permute-start.2) | collective-permute-done | bytes 23072 | tf_op jit(solution)/shard_map/ppermute | solution.py:301
  39.8 0.8 fusion.34
  40.8 0.8 fusion.41
  42.0 1.2 collective-permute-start.5
  43.2 0.8 collective-permute-start.6
  44.0 0.8 fusion.58
  44.9 1.7 collective-permute-done.5
  46.5 1.0 collective-permute-done.6
  47.6 0.6 copy-done.5
  48.3 0.7 reshape.467
  48.9 0.9 copy.59
  49.8 0.7 reshape.468
  50.5 2.6 %collective-permute-start.7 = (bf16[4,16,576]{2,1,0:T(8,128)(2,1)}, bf16[4,16,576]{2,1,0:T(8,128)(2,1)}, u32[]{:S(2)}, u32[]{:S(2)}) collective-permute-start(bf16[4,16,576]{2,1,0:T(8,128)(2,1)} %reshape.468), channel_id=1, source_target_pairs={{8,0},{16,8},{24,16},{0,24},{40,32},{48,40},{56,48},{32,56},{72,64... | collective-permute-start | bytes 221192 | tf_op jit(solution)/shard_map/ppermute | solution.py:305
  53.1 0.6 collective-permute-start.8
  53.7 0.6 collective-permute-start.9
  54.2 0.7 stack_reshape.3
  54.9 0.8 pad_maximum_fusion.7
  55.7 3.6 %collective-permute-start.14 = (bf16[4,4,576]{2,1,0:T(4,128)(2,1)S(1)}, bf16[4,4,576]{2,1,0:T(4,128)(2,1)S(1)}, u32[]{:S(2)}, u32[]{:S(2)}) collective-permute-start(bf16[4,4,576]{2,1,0:T(4,128)(2,1)S(1)} %pad_maximum_fusion.7), channel_id=1, source_target_pairs={{0,1},{1,0},{2,3},{3,2},{4,5},{5,4},{6,7},{7,6},{8,9},{9,8},{10,11... | collective-permute-start | bytes 55304 | tf_op jit(solution)/shard_map/ppermute | solution.py:297
  59.3 2.0 %fusion.57 = (bf16[1,4,4,16,576]{4,3,2,1,0:T(8,128)(2,1)}, bf16[4,4,16,576]{3,2,1,0:T(8,128)(2,1)}) fusion(bf16[1,4,16,576]{3,2,1,0:T(8,128)(2,1)} %bitcast.23, bf16[1,4,16,576]{3,2,1,0:T(8,128)(2,1)} %bitcast.22, bf16[1,4,16,576]{3,2,1,0:T(8,128)(2,1)} %bitcast.21, bf16[1,4,16,576]{3,2,1,0:T(8,128)(2,1)} %stack_reshape.3), kind=kLoop, calls=%fused_computation.119 | loop fusion | flops 442368 | bytes 884736 | tf_op jit(solution)/shard_map/stack | solution.py:420
  61.3 2.4 %collective-permute-start.10 = (bf16[4,4,16,576]{3,2,1,0:T(8,128)(2,1)}, bf16[4,4,16,576]{3,2,1,0:T(8,128)(2,1)}, u32[]{:S(2)}, u32[]{:S(2)}) collective-permute-start(bf16[4,4,16,576]{3,2,1,0:T(8,128)(2,1)} %get-tuple-element.21), channel_id=1, source_target_pairs={{32,0},{40,8},{48,16},{56,24},{64,32},{72,40},{80,48},{88,56},{96,... | collective-permute-start | bytes 884744 | tf_op jit(solution)/shard_map/ppermute | solution.py:311
  63.7 0.6 collective-permute-start.11
  64.2 0.6 collective-permute-start.12
  64.8 0.8 select_bitcast_fusion.1
  65.7 0.7 gather_fusion.1
  66.4 0.7 pad.4.rest_0_
  67.1 9.7 %collective-permute-done.10 = bf16[4,4,16,576]{3,2,1,0:T(8,128)(2,1)} collective-permute-done((bf16[4,4,16,576]{3,2,1,0:T(8,128)(2,1)}, bf16[4,4,16,576]{3,2,1,0:T(8,128)(2,1)}, u32[]{:S(2)}, u32[]{:S(2)}) %collective-permute-start.10) | collective-permute-done | bytes 294944 | tf_op jit(solution)/shard_map/ppermute | solution.py:311
  76.8 3.8 %collective-permute-done.11 = bf16[4,4,16,576]{3,2,1,0:T(8,128)(2,1)} collective-permute-done((bf16[4,4,16,576]{3,2,1,0:T(8,128)(2,1)}, bf16[4,4,16,576]{3,2,1,0:T(8,128)(2,1)}, u32[]{:S(2)}, u32[]{:S(2)}) %collective-permute-start.11) | collective-permute-done | bytes 294944 | tf_op jit(solution)/shard_map/ppermute | solution.py:311
  80.7 10.9 %collective-permute-done.12 = bf16[4,4,16,576]{3,2,1,0:T(8,128)(2,1)} collective-permute-done((bf16[4,4,16,576]{3,2,1,0:T(8,128)(2,1)}, bf16[4,4,16,576]{3,2,1,0:T(8,128)(2,1)}, u32[]{:S(2)}, u32[]{:S(2)}) %collective-permute-start.12) | collective-permute-done | bytes 294944 | tf_op jit(solution)/shard_map/ppermute | solution.py:311
  91.6 2.6 %pad_maximum_fusion.1 = bf16[4,4,4,16,576]{4,3,2,1,0:T(8,128)(2,1)} fusion(bf16[1,4,4,16,576]{4,3,2,1,0:T(8,128)(2,1)} %bitcast.27, bf16[1,4,4,16,576]{4,3,2,1,0:T(8,128)(2,1)} %bitcast.26, bf16[1,4,4,16,576]{4,3,2,1,0:T(8,128)(2,1)} %bitcast.25, bf16[1,4,4,16,576]{4,3,2,1,0:T(8,128)(2,1)} %get-tuple-element.20), kind=kLoop, calls=%fused_computation.10 | loop fusion | flops 1769472 | bytes 2359296 | tf_op jit(solution)/shard_map/stack | solution.py:420
  94.2 5.0 %collective-permute-start.13 = (bf16[16,4,16,576]{3,2,1,0:T(8,128)(2,1)}, bf16[16,4,16,576]{3,2,1,0:T(8,128)(2,1)}, u32[]{:S(2)}, u32[]{:S(2)}) collective-permute-start(bf16[16,4,16,576]{3,2,1,0:T(8,128)(2,1)} %bitcast.28), channel_id=1, source_target_pairs={{0,1},{1,0},{2,3},{3,2},{4,5},{5,4},{6,7},{7,6},{8,9},{9,8},{10,11... | collective-permute-start | bytes 3538952 | tf_op jit(solution)/shard_map/ppermute | solution.py:297
  99.5 0.7 convert_reduce_fusion.1
  101.1 0.7 select_reduce_fusion.order
  101.8 13.6 %attend_cache.1 = (bf16[32,32,512]{2,1,0:T(8,128)(2,1)}, bf16[32,32,128]{2,1,0:T(8,128)(2,1)}) custom-call(s32[32]{0:T(128)} %select_reduce_fusion.order, s32[32]{0:T(128)} %copy-done.11, s32[1]{0:T(128)} %bitcast.40.used, bf16[32,32,640]{2,1,0:T(8,128)(2,1)} %bitcast.105, bf16[32,576,384]{2,1,0:T(8,128)(2,1)} %bitcast.98, bf16[32,576,384]{2,1,0:T(8,128)(2,1)} %bitcast.99, ...), custom_call_target="tpu_custom_call" | custom-call | flops 3422552064 | bytes 14155776 | tf_op jit(solution)/shard_map/attend_cache/pallas_call | solution.py:242
  115.4 2.6 %fusion.23 = bf16[32,2,16,128]{3,0,1,2:T(8,128)(2,1)S(1)} fusion(bf16[16,512,128]{2,1,0:T(8,128)(2,1)S(1)} %copy-done, bf16[32,2,16,512]{3,2,1,0:T(8,128)(2,1)} %bitcast.110), kind=kOutput, calls=%fused_computation.16 | convolution fusion | flops 134348800 | bytes 3407872 | tf_op jit(solution)/shard_map/nshc,hcv->nshv/dot_general | solution.py:444
  118.2 0.9 pad_maximum_fusion.2
  119.1 4.6 %all-to-all-start.1 = ((bf16[16,64,256]{2,1,0:T(8,128)(2,1)}), bf16[16,64,256]{2,1,0:T(8,128)(2,1)S(1)}, u32[]{:S(2)}, u32[]{:S(2)}) async-start(bf16[16,64,256]{2,1,0:T(8,128)(2,1)} %pad_maximum_fusion.2), calls=%async_computation.1 | async-start | bytes 1048576 | tf_op jit(solution)/shard_map/all_to_all | solution.py:453
  123.7 3.6 %pad_maximum_fusion.group_ref = bf16[32,4,16,576]{3,2,1,0:T(8,128)(2,1)} fusion(bf16[16,4,16,576]{3,2,1,0:T(8,128)(2,1)} %collective-permute-done.13, bf16[16,4,16,576]{3,2,1,0:T(8,128)(2,1)} %bitcast.28), kind=kLoop, calls=%fused_computation.2 | loop fusion | flops 1179648 | bytes 4718592 | tf_op jit(solution)/shard_map/concatenate | solution.py:422
  127.3 27.6 %attend_prefill.1 = bf16[4,512,512]{2,1,0:T(8,128)(2,1)} custom-call(s32[5]{0:T(128)} %pad_add_fusion.info, bf16[4,512,576]{2,1,0:T(8,128)(2,1)} %bitcast.140, bf16[32,4,96,576]{3,2,1,0:T(8,128)(2,1)} %bitcast.102, bf16[32,4,16,576]{3,2,1,0:T(8,128)(2,1)} %pad_maximum_fusion.group_ref, s32[1,512]{1,0:T(1,128)} %add.395.token_ref), custom_call_target="tpu_custom_call" | custom-call | flops 18790481920 | bytes 21233664 | tf_op jit(solution)/shard_map/attend_prefill/pallas_call | solution.py:153
  154.9 10.2 %attend_decode.1 = (bf16[1,512,512]{2,1,0:T(8,128)(2,1)}, f32[1,512,128]{2,1,0:T(8,128)}) custom-call(s32[5]{0:T(128)} %pad_add_fusion.info, bf16[1,512,576]{2,1,0:T(8,128)(2,1)} %bitcast.108, bf16[32,4,96,576]{3,2,1,0:T(8,128)(2,1)} %bitcast.103, bf16[32,4,16,576]{3,2,1,0:T(8,128)(2,1)} %pad_maximum_fusion.group_ref, s32[1,512]{1,0:T(1,128)} %add.395.token_ref, ...), custom_call_target="tpu_custom_call" | custom-call | flops 4865392640 | bytes 5455872 | tf_op jit(solution)/shard_map/attend_decode/pallas_call | solution.py:153
  165.1 1.7 fusion.20
  166.9 0.9 copy.43
  167.7 2.5 %fusion.12 = bf16[4,32,16,128]{3,1,0,2:T(8,128)(2,1)S(1)} fusion(bf16[16,512,128]{2,1,0:T(8,128)(2,1)S(1)} %copy-done, bf16[4,32,16,512]{3,2,1,0:T(8,128)(2,1)S(1)} %bitcast.142), kind=kOutput, calls=%fused_computation.12 | convolution fusion | flops 268697600 | bytes 4718592 | tf_op jit(solution)/shard_map/pthc,hcv->pthv/dot_general | solution.py:497
  170.3 1.1 copy.44
  171.4 0.8 copy-done.3
  172.2 3.0 %merge_decode.1 = bf16[16,32,128]{2,1,0:T(8,128)(2,1)} custom-call(s32[16]{0:T(128)} %copy-done.12, bf16[32,32,256]{2,1,0:T(8,128)(2,1)} %bitcast.109, f32[16,32,128]{2,1,0:T(8,128)} %bitcast.111, f32[16,32,128]{2,1,0:T(8,128)} %bitcast.128), custom_call_target="tpu_custom_call" | custom-call | tf_op jit(solution)/shard_map/merge_decode/pallas_call | solution.py:286
  (81 shorter events, 3.5 us)
Async XLA Ops:
  7.2 108.3 %copy-start = (bf16[16,512,128]{2,1,0:T(8,128)(2,1)S(1)}, bf16[16,512,128]{2,1,0:T(8,128)(2,1)}, u32[]{:S(2)}) copy-start(bf16[16,512,128]{2,1,0:T(8,128)(2,1)} %param.23) | copy-start | bytes 6291460
  7.2 3.2 %copy-start.9 = (bf16[16,2,896]{2,1,0:T(2,128)(2,1)S(1)}, bf16[16,2,896]{2,1,0:T(2,128)(2,1)}, u32[]{:S(2)}) copy-start(bf16[16,2,896]{2,1,0:T(2,128)(2,1)} %param.16) | copy-start | bytes 172036
  7.2 120.1 %all-gather.3.cloned.1.call-start = ((), (), s32[]{:S(2)}) async-start(), calls=%async_computation.2 | async-start | bytes 16220160 | tf_op jit(solution)/shard_map/all_gather | solution.py:345
  9.2 5.3 %copy-start.14 = (s32[16,1]{0,1:T(1,128)S(1)}, s32[16,1]{0,1:T(1,128)}, u32[]{:S(2)}) copy-start(s32[16,1]{0,1:T(1,128)} %param.19) | copy-start | bytes 196
  9.2 6.0 %copy-start.1 = (s32[16]{0:T(128)S(1)}, s32[16]{0:T(128)}, u32[]{:S(2)}) copy-start(s32[16]{0:T(128)} %param.20) | copy-start | bytes 196
  12.3 0.7 copy-start.7
  13.0 17.2 %collective-permute-start = (bf16[4,20,576]{2,1,0:T(8,128)(2,1)S(1)}, bf16[4,20,576]{2,1,0:T(8,128)(2,1)}, u32[]{:S(2)}, u32[]{:S(2)}) collective-permute-start(bf16[4,20,576]{2,1,0:T(8,128)(2,1)S(1)} %dynamic-slice_bitcast_fusion), channel_id=1, source_target_pairs={{0,1},{1,0},{2,3},{3,2},{4,5},{5,4},{6,7},{7,6},{8,9},{9,8},{10,11... | collective-permute-start | bytes 276488 | tf_op jit(solution)/shard_map/ppermute | solution.py:297
  14.7 0.6 copy-start.12
  16.0 10.4 %copy-start.13 = (s32[4]{0:T(128)S(1)}, s32[4]{0:T(128)}, u32[]{:S(2)}) copy-start(s32[4]{0:T(128)} %param.15) | copy-start | bytes 52
  18.4 22.3 %copy-start.10 = (f32[512]{0:T(512)S(1)}, f32[512]{0:T(512)}, u32[]{:S(2)}) copy-start(f32[512]{0:T(512)} %param.22) | copy-start | bytes 6148
  18.4 80.8 %all-to-all-start = ((bf16[16,64,640]{2,1,0:T(8,128)(2,1)}), bf16[16,64,640]{2,1,0:T(8,128)(2,1)S(1)}, u32[]{:S(2)}, u32[]{:S(2)}) async-start(bf16[16,64,640]{2,1,0:T(8,128)(2,1)} %bitcast.106), calls=%async_computation | async-start | bytes 2621440 | tf_op jit(solution)/shard_map/all_to_all | solution.py:363
  31.9 5.4 %collective-permute-start.1 = (bf16[20,576]{1,0:T(8,128)(2,1)}, bf16[20,576]{1,0:T(8,128)(2,1)}, u32[]{:S(2)}, u32[]{:S(2)}) collective-permute-start(bf16[20,576]{1,0:T(8,128)(2,1)} %get-tuple-element.22), channel_id=1, source_target_pairs={{2,0},{4,2},{6,4},{0,6},{3,1},{5,3},{7,5},{1,7},{10,8},{12,10},{14... | collective-permute-start | bytes 69128 | tf_op jit(solution)/shard_map/ppermute | solution.py:301
  34.6 4.8 %collective-permute-start.2 = (bf16[20,576]{1,0:T(8,128)(2,1)}, bf16[20,576]{1,0:T(8,128)(2,1)}, u32[]{:S(2)}, u32[]{:S(2)}) collective-permute-start(bf16[20,576]{1,0:T(8,128)(2,1)} %get-tuple-element.24), channel_id=1, source_target_pairs={{4,0},{6,2},{0,4},{2,6},{5,1},{7,3},{1,5},{3,7},{12,8},{14,10},{8,... | collective-permute-start | bytes 69128 | tf_op jit(solution)/shard_map/ppermute | solution.py:301
  34.9 4.8 %collective-permute-start.3 = (bf16[20,576]{1,0:T(8,128)(2,1)}, bf16[20,576]{1,0:T(8,128)(2,1)}, u32[]{:S(2)}, u32[]{:S(2)}) collective-permute-start(bf16[20,576]{1,0:T(8,128)(2,1)} %get-tuple-element.23), channel_id=1, source_target_pairs={{6,0},{0,2},{2,4},{4,6},{7,1},{1,3},{3,5},{5,7},{14,8},{8,10},{10,... | collective-permute-start | bytes 69128 | tf_op jit(solution)/shard_map/ppermute | solution.py:301
  41.6 5.9 %copy-start.8 = (bf16[20,32]{1,0:T(8,128)(2,1)}, bf16[20,32]{1,0:T(8,128)(2,1)S(1)}, u32[]{:S(2)}) copy-start(bf16[20,32]{1,0:T(8,128)(2,1)S(1)} %get-tuple-element.26) | copy-start | bytes 3844
  41.7 3.2 %collective-permute-start.4 = (bf16[20,576]{1,0:T(8,128)(2,1)S(1)}, bf16[20,576]{1,0:T(8,128)(2,1)S(1)}, u32[]{:S(2)}, u32[]{:S(2)}) collective-permute-start(bf16[20,576]{1,0:T(8,128)(2,1)S(1)} %pad_maximum_fusion.6), channel_id=1, source_target_pairs={{2,0},{4,2},{6,4},{0,6},{3,1},{5,3},{7,5},{1,7},{10,8},{12,10},{14... | collective-permute-start | bytes 69128 | tf_op jit(solution)/shard_map/ppermute | solution.py:301
  42.0 4.5 %collective-permute-start.5 = (bf16[20,576]{1,0:T(8,128)(2,1)S(1)}, bf16[20,576]{1,0:T(8,128)(2,1)S(1)}, u32[]{:S(2)}, u32[]{:S(2)}) collective-permute-start(bf16[20,576]{1,0:T(8,128)(2,1)S(1)} %pad_maximum_fusion.6), channel_id=1, source_target_pairs={{4,0},{6,2},{0,4},{2,6},{5,1},{7,3},{1,5},{3,7},{12,8},{14,10},{8,... | collective-permute-start | bytes 69128 | tf_op jit(solution)/shard_map/ppermute | solution.py:301
  43.2 4.4 %collective-permute-start.6 = (bf16[20,576]{1,0:T(8,128)(2,1)S(1)}, bf16[20,576]{1,0:T(8,128)(2,1)S(1)}, u32[]{:S(2)}, u32[]{:S(2)}) collective-permute-start(bf16[20,576]{1,0:T(8,128)(2,1)S(1)} %pad_maximum_fusion.6), channel_id=1, source_target_pairs={{6,0},{0,2},{2,4},{4,6},{7,1},{1,3},{3,5},{5,7},{14,8},{8,10},{10,... | collective-permute-start | bytes 69128 | tf_op jit(solution)/shard_map/ppermute | solution.py:301
  46.5 1.0 copy-start.4
  47.6 0.6 copy-start.5
  50.5 8.8 %collective-permute-start.7 = (bf16[4,16,576]{2,1,0:T(8,128)(2,1)}, bf16[4,16,576]{2,1,0:T(8,128)(2,1)}, u32[]{:S(2)}, u32[]{:S(2)}) collective-permute-start(bf16[4,16,576]{2,1,0:T(8,128)(2,1)} %reshape.468), channel_id=1, source_target_pairs={{8,0},{16,8},{24,16},{0,24},{40,32},{48,40},{56,48},{32,56},{72,64... | collective-permute-start | bytes 221192 | tf_op jit(solution)/shard_map/ppermute | solution.py:305
  53.1 6.2 %collective-permute-start.8 = (bf16[4,16,576]{2,1,0:T(8,128)(2,1)}, bf16[4,16,576]{2,1,0:T(8,128)(2,1)}, u32[]{:S(2)}, u32[]{:S(2)}) collective-permute-start(bf16[4,16,576]{2,1,0:T(8,128)(2,1)} %reshape.468), channel_id=1, source_target_pairs={{16,0},{24,8},{0,16},{8,24},{48,32},{56,40},{32,48},{40,56},{80,64... | collective-permute-start | bytes 221192 | tf_op jit(solution)/shard_map/ppermute | solution.py:305
  53.7 5.7 %collective-permute-start.9 = (bf16[4,16,576]{2,1,0:T(8,128)(2,1)}, bf16[4,16,576]{2,1,0:T(8,128)(2,1)}, u32[]{:S(2)}, u32[]{:S(2)}) collective-permute-start(bf16[4,16,576]{2,1,0:T(8,128)(2,1)} %reshape.468), channel_id=1, source_target_pairs={{24,0},{0,8},{8,16},{16,24},{56,32},{32,40},{40,48},{48,56},{88,64... | collective-permute-start | bytes 221192 | tf_op jit(solution)/shard_map/ppermute | solution.py:305
  55.7 9.1 %collective-permute-start.14 = (bf16[4,4,576]{2,1,0:T(4,128)(2,1)S(1)}, bf16[4,4,576]{2,1,0:T(4,128)(2,1)S(1)}, u32[]{:S(2)}, u32[]{:S(2)}) collective-permute-start(bf16[4,4,576]{2,1,0:T(4,128)(2,1)S(1)} %pad_maximum_fusion.7), channel_id=1, source_target_pairs={{0,1},{1,0},{2,3},{3,2},{4,5},{5,4},{6,7},{7,6},{8,9},{9,8},{10,11... | collective-permute-start | bytes 55304 | tf_op jit(solution)/shard_map/ppermute | solution.py:297
  61.3 15.5 %collective-permute-start.10 = (bf16[4,4,16,576]{3,2,1,0:T(8,128)(2,1)}, bf16[4,4,16,576]{3,2,1,0:T(8,128)(2,1)}, u32[]{:S(2)}, u32[]{:S(2)}) collective-permute-start(bf16[4,4,16,576]{3,2,1,0:T(8,128)(2,1)} %get-tuple-element.21), channel_id=1, source_target_pairs={{32,0},{40,8},{48,16},{56,24},{64,32},{72,40},{80,48},{88,56},{96,... | collective-permute-start | bytes 884744 | tf_op jit(solution)/shard_map/ppermute | solution.py:311
  63.7 17.0 %collective-permute-start.11 = (bf16[4,4,16,576]{3,2,1,0:T(8,128)(2,1)}, bf16[4,4,16,576]{3,2,1,0:T(8,128)(2,1)}, u32[]{:S(2)}, u32[]{:S(2)}) collective-permute-start(bf16[4,4,16,576]{3,2,1,0:T(8,128)(2,1)} %get-tuple-element.21), channel_id=1, source_target_pairs={{64,0},{72,8},{80,16},{88,24},{96,32},{104,40},{112,48},{120,56},{... | collective-permute-start | bytes 884744 | tf_op jit(solution)/shard_map/ppermute | solution.py:311
  64.2 27.3 %collective-permute-start.12 = (bf16[4,4,16,576]{3,2,1,0:T(8,128)(2,1)}, bf16[4,4,16,576]{3,2,1,0:T(8,128)(2,1)}, u32[]{:S(2)}, u32[]{:S(2)}) collective-permute-start(bf16[4,4,16,576]{3,2,1,0:T(8,128)(2,1)} %get-tuple-element.21), channel_id=1, source_target_pairs={{96,0},{104,8},{112,16},{120,24},{0,32},{8,40},{16,48},{24,56},{32... | collective-permute-start | bytes 884744 | tf_op jit(solution)/shard_map/ppermute | solution.py:311
  94.2 29.5 %collective-permute-start.13 = (bf16[16,4,16,576]{3,2,1,0:T(8,128)(2,1)}, bf16[16,4,16,576]{3,2,1,0:T(8,128)(2,1)}, u32[]{:S(2)}, u32[]{:S(2)}) collective-permute-start(bf16[16,4,16,576]{3,2,1,0:T(8,128)(2,1)} %bitcast.28), channel_id=1, source_target_pairs={{0,1},{1,0},{2,3},{3,2},{4,5},{5,4},{6,7},{7,6},{8,9},{9,8},{10,11... | collective-permute-start | bytes 3538952 | tf_op jit(solution)/shard_map/ppermute | solution.py:297
  99.2 2.6 %copy-start.2 = (bf16[16,64,640]{2,1,0:T(8,128)(2,1)}, bf16[16,64,640]{2,1,0:T(8,128)(2,1)S(1)}, u32[]{:S(2)}) copy-start(bf16[16,64,640]{2,1,0:T(8,128)(2,1)S(1)} %all-to-all-done) | copy-start | bytes 3932164
  99.5 2.3 %copy-start.11 = (s32[32]{0:T(128)}, s32[32]{0:T(128)S(1)}, u32[]{:S(2)}) copy-start(s32[32]{0:T(128)S(1)} %fusion.45.length) | copy-start | bytes 388
  115.4 2.8 %copy-start.6 = (bf16[32,32,128]{2,1,0:T(8,128)(2,1)S(1)}, bf16[32,32,128]{2,1,0:T(8,128)(2,1)}, u32[]{:S(2)}) copy-start(bf16[32,32,128]{2,1,0:T(8,128)(2,1)} %get-tuple-element.7) | copy-start | bytes 786436
  119.1 52.3 %all-to-all-start.1 = ((bf16[16,64,256]{2,1,0:T(8,128)(2,1)}), bf16[16,64,256]{2,1,0:T(8,128)(2,1)S(1)}, u32[]{:S(2)}, u32[]{:S(2)}) async-start(bf16[16,64,256]{2,1,0:T(8,128)(2,1)} %pad_maximum_fusion.2), calls=%async_computation.1 | async-start | bytes 1048576 | tf_op jit(solution)/shard_map/all_to_all | solution.py:453
  165.1 2.6 %copy-start.15 = (bf16[4,512,512]{2,1,0:T(8,128)(2,1)S(1)}, bf16[4,512,512]{2,1,0:T(8,128)(2,1)}, u32[]{:S(2)}) copy-start(bf16[4,512,512]{2,1,0:T(8,128)(2,1)} %attend_prefill.1) | copy-start | bytes 6291460
  171.4 0.8 copy-start.3
Sparse Core Ops, SparseCore 0:
  10.9 100.6 all-gather.2

commit v2 on v1

--- a/solution.py
+++ b/solution.py
@@ -55,65 +55,35 @@
     return total
 
 
-def attend_body(shape, info, q_ref, past_ref, group_ref, token_ref, *rest):
-    tile, lat, factor, head_local, decode, chunk = shape
-    if decode:
-        fresh_ref, out_ref, lse_ref, hold = rest
-    else:
-        out_ref, hold = rest
+def attend_rows(shape, q_ref, out_ref, lse_ref, hold, past_keys, past_len, others, row_masks):
+    tile, lat, factor, chunk, past_count = shape
     rows = q_ref.shape[0]
-    pieces, piece_rows, width = past_ref.shape
-    step = chunk // piece_rows
-    past_count = pieces // step
-    past_total = pieces * piece_rows
-    half_past = past_total // 2
-    past_len = info[0] if decode else info[pl.program_id(0)]
-
-    def past_keys(j):
-        return past_ref[j * step : (j + 1) * step].reshape(chunk, width)
-
-    def group_keys():
-        return group_ref[...].reshape(group_ref.shape[0] * group_ref.shape[1], width)
-
-    group_total = group_ref.shape[0] * group_ref.shape[1]
     for i in range(rows // tile):
         span = pl.ds(i * tile, tile)
         queries = q_ref[span, :]
         row = lax.broadcasted_iota(jnp.int32, (tile, 1), 0) + i * tile
         highest = None
-        for j in range(past_count):
-            scores = key_scores(queries, past_keys(j), lat, NT)
-            if (j + 1) * chunk > half_past:
+        parts = []
+        end = 0
+        for j in range(past_count + len(others)):
+            keys = functools.partial(past_keys, j) if j < past_count else others[j - past_count]
+            block = keys()
+            scores = key_scores(queries, block, lat, NT)
+            if j >= past_count:
+                mask = row_masks[j - past_count](row)
+                if mask is not None:
+                    scores = jnp.where(mask, scores, negative)
+            elif (j + 1) * chunk > past_count * chunk // 2:
                 place = lax.broadcasted_iota(jnp.int32, (1, chunk), 1) + j * chunk
                 scores = jnp.where(place < past_len, scores, negative)
-            hold[i % 2, :, j * chunk : (j + 1) * chunk] = scores
-            highest = lane_fold(jnp.maximum, highest, scores)
-        scores = key_scores(queries, group_keys(), lat, NT)
-        if not decode:
-            token = info[4] + row // head_local
-            scores = jnp.where(token_ref[...] <= token, scores, negative)
-        hold[i % 2, :, past_total : past_total + group_total] = scores
-        highest = lane_fold(jnp.maximum, highest, scores)
-        if decode:
-            fresh = fresh_ref[...]
-            scores = key_scores(queries, fresh, lat, NT)
-            place = lax.broadcasted_iota(jnp.int32, (1, fresh.shape[0]), 1)
-            request = row // (2 * head_local)
-            last = row // head_local
-            scores = jnp.where((place >= 2 * request) & (place <= last), scores, negative)
-            fresh_span = slice(past_total + group_total, past_total + group_total + fresh.shape[0])
-            hold[i % 2, :, fresh_span] = scores
+            place = slice(end, end + block.shape[0])
+            end += block.shape[0]
+            parts.append((place, keys))
+            hold[i % 2, :, place] = scores
             highest = lane_fold(jnp.maximum, highest, scores)
         peak = jnp.max(highest, axis=1, keepdims=True)
         total = None
         summed = None
-        parts = [
-            (slice(j * chunk, (j + 1) * chunk), functools.partial(past_keys, j))
-            for j in range(past_count)
-        ]
-        parts.append((slice(past_total, past_total + group_total), group_keys))
-        if decode:
-            parts.append((fresh_span, lambda: fresh_ref[...]))
         for place, keys in parts:
             weights = jnp.exp2((hold[i % 2, :, place] - peak) * factor)
             total = lane_fold(jnp.add, total, weights)
@@ -121,53 +91,188 @@
             summed = part if summed is None else summed + part
         total = jnp.sum(total, axis=1, keepdims=True)
         out_ref[span, :] = (summed / total).astype(jnp.bfloat16)
-        if decode:
+        if lse_ref is not None:
             lse = peak * factor + jnp.log2(total)
             lse_ref[span, :] = jnp.broadcast_to(lse, (tile, lse_ref.shape[1]))
 
 
-def attend(info, query, past, group, token, fresh, lat, factor, head_local):
-    decode = fresh is not None
-    count, rows, width = query.shape
+def group_masks(info, token_ref, head_local):
+    def mask(c):
+        return lambda row: token_ref[c : c + 1, :] <= info[4] + row // head_local
+
+    return [mask(0), mask(1)]
+
+
+def later_body(
+    shape, head_local, first, info, q_ref, past_ref, near_ref, far_ref, token_ref, out_ref, hold
+):
+    chunk, past_count = shape[3:]
+    pieces, piece_rows, width = past_ref.shape
+    step = pieces // past_count
+
+    def past_keys(j):
+        return past_ref[j * step : (j + 1) * step].reshape(chunk, width)
+
+    attend_rows(
+        shape,
+        q_ref,
+        out_ref,
+        None,
+        hold,
+        past_keys,
+        info[first + pl.program_id(0)],
+        [lambda: near_ref[...], lambda: far_ref[...]],
+        group_masks(info, token_ref, head_local),
+    )
+
+
+def first_body(
+    shape, head_local, pieces, info, q_ref, dq_ref, near_ref, far_ref, token_ref, fresh_ref, *rest
+):
+    chunk, past_count = shape[3:]
+    piece_refs = rest[:pieces]
+    out_ref, decode_ref, lse_ref, hold, past, arrive = rest[pieces:]
+    holders, piece_rows, width = past.shape
+    step = holders // past_count
+    z_place, x_place, core = info[6], info[7], info[8]
+    copies = []
+    for c in range(2):
+        side = core if c == 0 else 1 - core
+        for dz in range(4):
+            for dx in range(4):
+                holder = lax.rem(z_place + dz, 4) * 4 + lax.rem(x_place + dx, 4)
+                copies.append(
+                    pltpu.make_async_copy(
+                        piece_refs[c * 4 + dz].at[dx],
+                        past.at[holder * 2 + side],
+                        arrive.at[c * 16 + dz * 4 + dx],
+                    )
+                )
+    for copy in copies:
+        copy.start()
+    for copy in copies:
+        copy.wait()
+
+    def past_keys(j):
+        return past[j * step : (j + 1) * step].reshape(chunk, width)
+
+    group = [lambda: near_ref[...], lambda: far_ref[...]]
+    attend_rows(
+        shape,
+        q_ref,
+        out_ref,
+        None,
+        hold,
+        past_keys,
+        info[0],
+        group,
+        group_masks(info, token_ref, head_local),
+    )
+
+    def fresh_mask(row):
+        place = lax.broadcasted_iota(jnp.int32, (1, fresh_ref.shape[0]), 1)
+        return (place >= row // (2 * head_local) * 2) & (place <= row // head_local)
+
+    attend_rows(
+        shape,
+        dq_ref,
+        decode_ref,
+        lse_ref,
+        hold,
+        past_keys,
+        info[0],
+        group + [lambda: fresh_ref[...]],
+        [lambda row: None, lambda row: None, fresh_mask],
+    )
+
+
+def attend_later(info, query, past, near, far, token, first, lat, factor, head_local):
+    count = past.shape[1]
+    _, rows, width = query.shape
     pieces, _, piece_rows, _ = past.shape
-    group_pieces, _, group_rows, _ = group.shape
-    keys = pieces * piece_rows + group_pieces * group_rows
+    keys = pieces * piece_rows + 2 * near.shape[1]
     tile = min(256, rows)
     chunk = 768
-    in_specs = [
-        pl.BlockSpec((None, rows, width), lambda p, _: (p, 0, 0)),
-        pl.BlockSpec((pieces, None, piece_rows, width), lambda p, _: (0, p, 0, 0)),
-        pl.BlockSpec((group_pieces, None, group_rows, width), lambda p, _: (0, p, 0, 0)),
-        pl.BlockSpec(token.shape, lambda p, _: (0, 0)),
-    ]
-    operands = [query, past, group, token]
-    out_specs = [pl.BlockSpec((None, rows, lat), lambda p, _: (p, 0, 0))]
-    out_shape = [jax.ShapeDtypeStruct((count, rows, lat), jnp.bfloat16)]
-    if decode:
-        in_specs.append(pl.BlockSpec(fresh.shape, lambda p, _: (0, 0)))
-        operands.append(fresh)
-        keys += fresh.shape[0]
-        out_specs.append(pl.BlockSpec((None, rows, 128), lambda p, _: (p, 0, 0)))
-        out_shape.append(jax.ShapeDtypeStruct((count, rows, 128), jnp.float32))
-    shape = (tile, lat, factor, head_local, decode, chunk)
+    shape = (tile, lat, factor, chunk, pieces * piece_rows // chunk)
+
+    def group_place(p, info):
+        return (lax.rem(p + first + info[5], 4), 0, 0)
+
+    group_spec = pl.BlockSpec((None, near.shape[1], width), group_place)
     return pl.pallas_call(
-        functools.partial(attend_body, shape),
+        functools.partial(later_body, shape, head_local, first),
         grid_spec=pltpu.PrefetchScalarGridSpec(
             num_scalar_prefetch=1,
             grid=(count,),
-            in_specs=in_specs,
-            out_specs=out_specs,
+            in_specs=[
+                pl.BlockSpec((None, rows, width), lambda p, _: (p + first, 0, 0)),
+                pl.BlockSpec((pieces, None, piece_rows, width), lambda p, _: (0, p, 0, 0)),
+                group_spec,
+                group_spec,
+                pl.BlockSpec(token.shape, lambda p, _: (0, 0)),
+            ],
+            out_specs=pl.BlockSpec((None, rows, lat), lambda p, _: (p, 0, 0)),
             scratch_shapes=[pltpu.VMEM((2, tile, keys), jnp.float32)],
         ),
-        out_shape=out_shape,
+        out_shape=jax.ShapeDtypeStruct((count, rows, lat), jnp.bfloat16),
         compiler_params=pltpu.CompilerParams(vmem_limit_bytes=VMEM_BYTES),
         cost_estimate=pl.CostEstimate(
             flops=2 * count * rows * keys * (768 + lat),
             bytes_accessed=2 * count * (keys + 2 * rows) * width,
             transcendentals=count * rows * keys,
         ),
-        name="attend_decode" if decode else "attend_prefill",
-    )(info, *operands)
+        name="attend_later",
+    )(info, query, past, near, far, token)
+
+
+def attend_first(info, query, decode_query, past, near, far, token, fresh, lat, factor, head_local):
+    _, rows, width = query.shape
+    decode_rows = decode_query.shape[0]
+    holders = 2 * 16
+    piece_rows = past[0].shape[1]
+    keys = holders * piece_rows + 2 * near.shape[1] + fresh.shape[0]
+    tile = min(256, rows)
+    chunk = 768
+    shape = (tile, lat, factor, chunk, holders * piece_rows // chunk)
+    group_spec = pl.BlockSpec((None, near.shape[1], width), lambda p, info: (info[5], 0, 0))
+    return pl.pallas_call(
+        functools.partial(first_body, shape, head_local, len(past)),
+        grid_spec=pltpu.PrefetchScalarGridSpec(
+            num_scalar_prefetch=1,
+            grid=(1,),
+            in_specs=[
+                pl.BlockSpec((None, rows, width), lambda p, _: (0, 0, 0)),
+                pl.BlockSpec(decode_query.shape, lambda p, _: (0, 0)),
+                group_spec,
+                group_spec,
+                pl.BlockSpec(token.shape, lambda p, _: (0, 0)),
+                pl.BlockSpec(fresh.shape, lambda p, _: (0, 0)),
+            ]
+            + [pl.BlockSpec(memory_space=pl.ANY)] * len(past),
+            out_specs=[
+                pl.BlockSpec((None, rows, lat), lambda p, _: (0, 0, 0)),
+                pl.BlockSpec((decode_rows, lat), lambda p, _: (0, 0)),
+                pl.BlockSpec((decode_rows, 128), lambda p, _: (0, 0)),
+            ],
+            scratch_shapes=[
+                pltpu.VMEM((2, tile, keys), jnp.float32),
+                pltpu.VMEM((holders, piece_rows, width), jnp.bfloat16),
+                pltpu.SemaphoreType.DMA((32,)),
+            ],
+        ),
+        out_shape=[
+            jax.ShapeDtypeStruct((1, rows, lat), jnp.bfloat16),
+            jax.ShapeDtypeStruct((decode_rows, lat), jnp.bfloat16),
+            jax.ShapeDtypeStruct((decode_rows, 128), jnp.float32),
+        ],
+        compiler_params=pltpu.CompilerParams(vmem_limit_bytes=VMEM_BYTES),
+        cost_estimate=pl.CostEstimate(
+            flops=2 * (rows + decode_rows) * keys * (768 + lat),
+            bytes_accessed=2 * (keys + 2 * rows + 2 * decode_rows) * width,
+            transcendentals=(rows + decode_rows) * keys,
+        ),
+        name="attend_first",
+    )(info, query, decode_query, near, far, token, fresh, *past)
 
 
 def dispatch_body(source, length, q_ref, out_ref):
@@ -177,7 +282,7 @@
     for slot in range(slots):
         out_ref[slot, :, :lat_rope] = q_ref[source[slot]]
         size = length[slot]
-        tail = jnp.where(lane < 32, size // 16, size % 16)
+        tail = jnp.where(lane < 32, size >> 4, size & 15)
         out_ref[slot, :, lat_rope:] = tail.astype(jnp.float32).astype(jnp.bfloat16)
 
 
@@ -329,7 +434,7 @@
     seq_place = lax.axis_index("seq")
     tp_place = lax.axis_index("tp")
     core = lax.axis_index("grp")
-    z_place, x_place = seq_place // 4, seq_place % 4
+    z_place, x_place = seq_place >> 2, seq_place & 3
     prompt_count, group_local, head_local, row_width = group_query.shape
     past_local = past_cache.shape[1]
     request_local = decode_query.shape[0]
@@ -342,7 +447,11 @@
 
     half = past_local // 2
     past_half = lax.dynamic_slice_in_dim(past_cache, core * half, half, axis=1)
-    past_all = lax.all_gather(past_half, ("seq", "grp"), axis=0, tiled=False)
+    past_later = lax.all_gather(past_half[1:], ("seq", "grp"), axis=0, tiled=False)
+    past_x = [past_half[0]] + [fetch_x(past_half[0], shift) for shift in range(1, 4)]
+    past_x = jnp.stack(past_x)
+    past_first = [past_x] + [fetch_z(past_x, shift) for shift in range(1, 4)]
+    past_first = past_first + [swap_core(piece) for piece in past_first]
 
     targets = owner[:, 0]
     request_order = jnp.arange(request_local, dtype=jnp.int32)
@@ -370,64 +479,62 @@
     marks = arrived[:, 0, row_width:].astype(jnp.float32)
     slot_length = (marks[:, 0] * 16 + marks[:, 32]).astype(jnp.int32)
 
-    part_tokens = group_local // 8
-    part_pairs = 2 * request_local // 8
-    part_rows = prompt_count * part_tokens + part_pairs
-    hidden_group = group_hidden.reshape(prompt_count, 8, part_tokens, -1).transpose(1, 0, 2, 3)
-    hidden_decode = decode_hidden.reshape(8, part_pairs, -1)
-    hidden = jnp.concatenate(
-        [hidden_group.reshape(8, prompt_count * part_tokens, -1), hidden_decode], axis=1
-    )
-    partial = jnp.einsum("krd,dc->krc", hidden, w_latent, preferred_element_type=jnp.float32)
-    partial = partial.astype(jnp.bfloat16).reshape(4, 2, part_rows, row_width)
-    keep = lax.dynamic_index_in_dim(partial, core, axis=1, keepdims=False)
-    give = lax.dynamic_index_in_dim(partial, 1 - core, axis=1, keepdims=False)
-    pair_sum = (keep.astype(jnp.float32) + swap_core(give).astype(jnp.float32)).astype(jnp.bfloat16)
-    latent = lax.dynamic_index_in_dim(pair_sum, tp_place, axis=0, keepdims=False)
-    latent = latent.astype(jnp.float32)
+    half_tokens = group_local // 2
+    pairs = 2 * request_local
+    partial_group = jnp.einsum(
+        "ptd,dc->ptc", group_hidden, w_latent, preferred_element_type=jnp.float32
+    ).astype(jnp.bfloat16)
+    partial_group = partial_group.reshape(prompt_count, 2, half_tokens, row_width)
+    partial_decode = jnp.einsum(
+        "rd,dc->rc",
+        decode_hidden.reshape(pairs, -1),
+        w_latent,
+        preferred_element_type=jnp.float32,
+    ).astype(jnp.bfloat16)
+    keep = lax.dynamic_index_in_dim(partial_group, core, axis=1, keepdims=False)
+    give = lax.dynamic_index_in_dim(partial_group, 1 - core, axis=1, keepdims=False)
+    taken = swap_core(
+        jnp.concatenate([give.reshape(prompt_count * half_tokens, row_width), partial_decode])
+    ).astype(jnp.float32)
+    sum_group = keep.astype(jnp.float32) + taken[: prompt_count * half_tokens].reshape(keep.shape)
+    sum_decode = partial_decode.astype(jnp.float32) + taken[prompt_count * half_tokens :]
+    sum_group = sum_group.astype(jnp.bfloat16)
+    sum_decode = sum_decode.astype(jnp.bfloat16)
+
+    def part_of(place):
+        chosen = lax.dynamic_index_in_dim(sum_group, place & 3, axis=0, keepdims=False)
+        return jnp.concatenate([chosen, sum_decode])
+
+    latent = part_of(tp_place).astype(jnp.float32)
     for shift in range(1, 4):
-        sent = lax.dynamic_index_in_dim(
-            pair_sum, (tp_place - shift) % 4, axis=0, keepdims=False
-        )
-        latent = latent + fetch_tp(sent, shift).astype(jnp.float32)
-    part = tp_place * 2 + core
-    token = part * part_tokens + jnp.arange(part_tokens, dtype=jnp.int32)
-    group_positions = past_len[:, None] + seq_place * group_local + token[None, :]
-    pair_index = part * part_pairs + jnp.arange(part_pairs, dtype=jnp.int32)
+        latent = latent + fetch_tp(part_of(tp_place - shift), shift).astype(jnp.float32)
+    half_order = jnp.arange(half_tokens, dtype=jnp.int32)
+    group_positions = (
+        past_len[tp_place] + seq_place * group_local + core * half_tokens + half_order
+    )
+    pair_order = jnp.arange(pairs, dtype=jnp.int32)
     decode_positions = (
-        past_len[0] + group_local * seq_count + dec_len[pair_index // 2] + pair_index % 2
-    )
-    positions = jnp.concatenate([group_positions.reshape(-1), decode_positions])
+        past_len[0]
+        + group_local * seq_count
+        + (dec_len[:, None] + jnp.arange(2, dtype=jnp.int32)).reshape(-1)
+    )
+    positions = jnp.concatenate([group_positions, decode_positions])
     rows_own = make_rows(latent, kv_gain, positions)
-    rows_tp = [rows_own] + [fetch_tp(rows_own, shift) for shift in range(1, 4)]
-    tp_order = (tp_place + jnp.arange(4, dtype=jnp.int32)) % 4
-    rows_tp = jnp.stack(rows_tp)
-
-    fresh_own = rows_tp[:, prompt_count * part_tokens :]
-    fresh_other = swap_core(fresh_own)
-    fresh_even = jnp.where(core == 0, fresh_own, fresh_other)
-    fresh_odd = jnp.where(core == 0, fresh_other, fresh_own)
-    fresh = jnp.stack([fresh_even, fresh_odd], axis=1)
-    fresh = fresh[(jnp.arange(4, dtype=jnp.int32) - tp_place) % 4]
-    fresh = fresh.reshape(2 * request_local, row_width)
-    fresh = jnp.pad(fresh, ((0, 128 - 2 * request_local), (0, 0)))
-
-    group_own = rows_tp[:, : prompt_count * part_tokens].reshape(
-        4, prompt_count, part_tokens, row_width
-    )
-    group_own = group_own.transpose(1, 0, 2, 3).reshape(prompt_count, 4 * part_tokens, row_width)
+    fresh = jnp.pad(rows_own[half_tokens:], ((0, 128 - pairs), (0, 0)))
+
+    group_own = rows_own[:half_tokens]
     group_x = jnp.stack([group_own] + [fetch_x(group_own, shift) for shift in range(1, 4)])
     group_z = jnp.stack([group_x] + [fetch_z(group_x, shift) for shift in range(1, 4)])
-    group_z = group_z.reshape(16, prompt_count, 4 * part_tokens, row_width)
-    group_all = jnp.concatenate([group_z, swap_core(group_z)], axis=0)
+    group_z = group_z.reshape(seq_count * half_tokens, row_width)
+    group_near = jnp.stack([group_z] + [fetch_tp(group_z, shift) for shift in range(1, 4)])
+    group_far = swap_core(group_near)
     ring = jnp.arange(4, dtype=jnp.int32)
-    holder = ((z_place + ring) % 4)[:, None] * 4 + ((x_place + ring) % 4)[None, :]
-    cores = jnp.stack([core, 1 - core])
-    key_token = (
-        holder.reshape(1, 16, 1, 1) * group_local
-        + (tp_order.reshape(1, 1, 4, 1) * 2 + cores.reshape(2, 1, 1, 1)) * part_tokens
-        + jnp.arange(part_tokens, dtype=jnp.int32).reshape(1, 1, 1, part_tokens)
-    ).reshape(1, seq_count * group_local)
+    holder = ((z_place + ring) & 3)[:, None] * 4 + ((x_place + ring) & 3)[None, :]
+    key_token = holder.reshape(seq_count, 1) * group_local + half_order[None, :]
+    key_token = key_token.reshape(1, seq_count * half_tokens)
+    key_token = jnp.concatenate(
+        [key_token + core * half_tokens, key_token + (1 - core) * half_tokens], axis=0
+    )
 
     is_used = slot_length > 0
     used_rank = jnp.cumsum(is_used.astype(jnp.int32)) - 1
@@ -458,12 +565,18 @@
         tiled=True,
     ).reshape(slot_count, query_pairs, 2 * value_width)
 
-    info = jnp.concatenate([past_len, (seq_place * group_local)[None]]).astype(jnp.int32)
-    near_latent, near_lse = attend(
+    info = jnp.stack(
+        [past_len[p] for p in range(prompt_count)]
+        + [seq_place * group_local, (4 - tp_place) & 3, z_place, x_place, core]
+    ).astype(jnp.int32)
+    queries = group_query.reshape(prompt_count, group_local * head_local, row_width)
+    first_latent, near_latent, near_lse = attend_first(
         info,
-        decode_query.reshape(1, request_local * query_pairs, row_width),
-        past_all,
-        group_all,
+        queries,
+        decode_query.reshape(request_local * query_pairs, row_width),
+        past_first,
+        group_near,
+        group_far,
         key_token,
         fresh,
         lat,
@@ -483,17 +596,10 @@
         near_lse.reshape(request_local, query_pairs, 128),
     ).reshape(request_local, 2, head_local, value_width)
 
-    (prefill_latent,) = attend(
-        info,
-        group_query.reshape(prompt_count, group_local * head_local, row_width),
-        past_all,
-        group_all,
-        key_token,
-        None,
-        lat,
-        factor,
-        head_local,
-    )
+    later_latent = attend_later(
+        info, queries, past_later, group_near, group_far, key_token, 1, lat, factor, head_local
+    )
+    prefill_latent = jnp.concatenate([first_latent, later_latent], axis=0)
     prefill_out = jnp.einsum(
         "pthc,hcv->pthv",
         prefill_latent.reshape(prompt_count, group_local, head_local, lat),

time: 183 us -> 194 us (1.060)
  starting transfers between devices: 35.9 us -> 61.1 us
  other arithmetic: 20.2 us -> 13.4 us
  waiting for transfers between devices: 29.8 us -> 24.4 us
  Pallas kernels: 56.9 us -> 53.5 us
    ppermute x3 -> x6, waiting for transfers between devices: 24.5 us -> 9.62 us  [fetch_z(): lax.ppermute(value, 'seq', [((i + 4 * shift) % 16, i) for i in range(16)])]
    ppermute x3 -> x6, starting transfers between devices: 3.73 us -> 17 us  [fetch_x(): lax.ppermute(value, 'seq', [(i // 4 * 4 + (i + shift) % 4, i) for i in ra...]
    ppermute x3 -> x6, waiting for transfers between devices: 0.01 us -> 7.18 us  [fetch_x(): lax.ppermute(value, 'seq', [(i // 4 * 4 + (i + shift) % 4, i) for i in ra...]
    ppermute x3 -> x6, starting transfers between devices: 10.1 us -> 15.9 us  [swap_core(): return lax.ppermute(value, 'grp', [(0, 1), (1, 0)])]
    pallas_call x1, Pallas kernels: 13.6 us -> 9 us  [attend_cache(): pl.pallas_call(functools.partial(cache_body, lat, factor, batch), grid_sp...]
    ppermute x3 -> x6, starting transfers between devices: 3.55 us -> 8.12 us  [fetch_z(): lax.ppermute(value, 'seq', [((i + 4 * shift) % 16, i) for i in range(16)])]
    another operation x2, other arithmetic: 4.59 us -> 1.54 us  [on_device(): jnp.stack([group_x] + [fetch_z(group_x, shift) for shift in range(1, 4)])]
    another operation x7 -> x5, other arithmetic: 1.95 us -> 4.81 us  [the longest x1 2.58 us: on_device(): jnp.stack([group_z] + [fetch_tp(group_z, shift) for shift in range(1, 4)])]
  transfers between devices with their start and end apart: 18 -> 27, of which waited for: 8 -> 6; matrix products, arithmetic and copies ran while one was open for 22% -> 15% of each run, Pallas kernels for 30% -> 16%
where the time goes in v2:
time: 194 us; the launch traced here: 192 us
  starting transfers between devices  61.1 us (31%)
  Pallas kernels  53.5 us (28%)
  waiting for transfers between devices  24.4 us (13%)
  between operations  16.3 us (8%)
  local copies, waits for them, and re-layouts  14.8 us (8%)
  other arithmetic  13.4 us (7%)
  matrix products  8.99 us (5%)
    pallas_call x1, Pallas kernels, attend_later(): pl.pallas_call(functools.partial(later_body, shape, head_local, first), g...  22.2 us
    ppermute x6, starting transfers between devices, fetch_x(): lax.ppermute(value, 'seq', [(i // 4 * 4 + (i + shift) % 4, i) for i in ra...  17 us
    pallas_call x1, Pallas kernels, attend_first(): pl.pallas_call(functools.partial(first_body, shape, head_local, len(past)...  17 us
    ppermute x6, starting transfers between devices, swap_core(): return lax.ppermute(value, 'grp', [(0, 1), (1, 0)])  15.9 us
    ppermute x6, waiting for transfers between devices, fetch_z(): lax.ppermute(value, 'seq', [((i + 4 * shift) % 16, i) for i in range(16)])  9.62 us
    pallas_call x1, Pallas kernels, attend_cache(): pl.pallas_call(functools.partial(cache_body, lat, factor, batch), grid_sp...  9 us
    ppermute x6, starting transfers between devices, fetch_z(): lax.ppermute(value, 'seq', [((i + 4 * shift) % 16, i) for i in range(16)])  8.12 us
    ppermute x6, waiting for transfers between devices, fetch_tp(): return lax.ppermute(value, 'tp', [((i + shift) % 4, i) for i in range(4)])  7.51 us
  transfers between devices with their start and end apart: 27, of which 6 were waited for; matrix products, arithmetic and copies ran while one was open for 15% of the time, Pallas kernels for 16%

profile of v2, /device:TPU:1, one launch (start us, length us, event | category | flops | bytes accessed | tf_op | source)
XLA Modules:
  0.0 192.5 jit_solution(16801984814180738237)
XLA Ops:
  7.3 1.9 %constant_dynamic-slice_fusion.1 = bf16[3,96,576]{2,1,0:T(8,128)(2,1)} fusion(bf16[4,192,576]{2,1,0:T(8,128)(2,1)} %param.14, s32[]{:T(128)S(6)} %add.281, s32[]{:T(128)S(6)} %select_n.44), kind=kLoop, calls=%fused_computation.77 | loop fusion | bytes 663560 | tf_op jit(solution)/shard_map/slice | solution.py:450
  9.2 1.6 fusion.54
  10.8 2.0 %collective-permute-start.16 = (bf16[96,576]{1,0:T(8,128)(2,1)}, bf16[96,576]{1,0:T(8,128)(2,1)}, u32[]{:S(2)}, u32[]{:S(2)}) collective-permute-start(bf16[96,576]{1,0:T(8,128)(2,1)} %fusion.54), channel_id=1, source_target_pairs={{24,0},{0,8},{8,16},{16,24},{56,32},{32,40},{40,48},{48,56},{88,64... | collective-permute-start | bytes 331784 | tf_op jit(solution)/shard_map/ppermute | solution.py:410
  12.8 2.5 %collective-permute-start.15 = (bf16[96,576]{1,0:T(8,128)(2,1)}, bf16[96,576]{1,0:T(8,128)(2,1)}, u32[]{:S(2)}, u32[]{:S(2)}) collective-permute-start(bf16[96,576]{1,0:T(8,128)(2,1)} %fusion.54), channel_id=1, source_target_pairs={{16,0},{24,8},{0,16},{8,24},{48,32},{56,40},{32,48},{40,56},{80,64... | collective-permute-start | bytes 331784 | tf_op jit(solution)/shard_map/ppermute | solution.py:410
  15.3 0.8 reshape.239
  16.1 1.8 convolution_convert_fusion
  18.0 0.4 convolution_convert_fusion.1
  18.4 1.3 collective-permute-start
  19.8 0.6 fusion.50
  21.8 0.2 convert_reduce_fusion
  22.2 1.4 collective-permute-start.3
  23.5 2.6 %collective-permute-start.2 = (bf16[48,576]{1,0:T(8,128)(2,1)S(1)}, bf16[48,576]{1,0:T(8,128)(2,1)S(1)}, u32[]{:S(2)}, u32[]{:S(2)}) collective-permute-start(bf16[48,576]{1,0:T(8,128)(2,1)S(1)} %get-tuple-element.31), channel_id=1, source_target_pairs={{4,0},{6,2},{0,4},{2,6},{5,1},{7,3},{1,5},{3,7},{12,8},{14,10},{8,... | collective-permute-start | bytes 165896 | tf_op jit(solution)/shard_map/ppermute | solution.py:406
  26.1 1.1 collective-permute-start.1
  27.3 2.3 %collective-permute-done.2 = bf16[48,576]{1,0:T(8,128)(2,1)S(1)} collective-permute-done((bf16[48,576]{1,0:T(8,128)(2,1)S(1)}, bf16[48,576]{1,0:T(8,128)(2,1)S(1)}, u32[]{:S(2)}, u32[]{:S(2)}) %collective-permute-start.2) | collective-permute-done | bytes 55328 | tf_op jit(solution)/shard_map/ppermute | solution.py:406
  29.8 0.2 fusion.41
  30.2 2.3 %collective-permute-start.5 = (bf16[16,576]{1,0:T(8,128)(2,1)S(1)}, bf16[16,576]{1,0:T(8,128)(2,1)S(1)}, u32[]{:S(2)}, u32[]{:S(2)}) collective-permute-start(bf16[16,576]{1,0:T(8,128)(2,1)S(1)} %pad_maximum_fusion.11), channel_id=1, source_target_pairs={{16,0},{24,8},{0,16},{8,24},{48,32},{56,40},{32,48},{40,56},{80,64... | collective-permute-start | bytes 55304 | tf_op jit(solution)/shard_map/ppermute | solution.py:410
  32.5 0.3 collective-permute-start.4
  32.8 0.6 select_reduce_fusion.1
  33.4 2.4 %dispatch_queries.1 = bf16[32,32,640]{2,1,0:T(8,128)(2,1)} custom-call(s32[32]{0:T(128)} %get-tuple-element.21.source, s32[32]{0:T(128)} %get-tuple-element.20.length, bf16[16,32,576]{2,1,0:T(8,128)(2,1)} %bitcast.107), custom_call_target="tpu_custom_call" | custom-call | tf_op jit(solution)/shard_map/dispatch_queries/pallas_call | solution.py:294
  35.8 7.2 %all-to-all-start = ((bf16[16,64,640]{2,1,0:T(8,128)(2,1)}), bf16[16,64,640]{2,1,0:T(8,128)(2,1)S(1)}, u32[]{:S(2)}, u32[]{:S(2)}) async-start(bf16[16,64,640]{2,1,0:T(8,128)(2,1)} %bitcast.101), calls=%async_computation | async-start | bytes 2621440 | tf_op jit(solution)/shard_map/all_to_all | solution.py:472
  43.0 0.8 fusion.49
  43.8 1.4 collective-permute-start.9
  45.2 2.4 %collective-permute-start.8 = (bf16[4,16,576]{2,1,0:T(8,128)(2,1)S(1)}, bf16[4,16,576]{2,1,0:T(8,128)(2,1)S(1)}, u32[]{:S(2)}, u32[]{:S(2)}) collective-permute-start(bf16[4,16,576]{2,1,0:T(8,128)(2,1)S(1)} %get-tuple-element.25), channel_id=1, source_target_pairs={{64,0},{72,8},{80,16},{88,24},{96,32},{104,40},{112,48},{120,56},{... | collective-permute-start | bytes 221192 | tf_op jit(solution)/shard_map/ppermute | solution.py:416
  47.6 1.2 collective-permute-start.7
  48.8 3.9 %collective-permute-done.9 = bf16[4,16,576]{2,1,0:T(8,128)(2,1)S(1)} collective-permute-done((bf16[4,16,576]{2,1,0:T(8,128)(2,1)S(1)}, bf16[4,16,576]{2,1,0:T(8,128)(2,1)S(1)}, u32[]{:S(2)}, u32[]{:S(2)}) %collective-permute-start.9) | collective-permute-done | bytes 73760 | tf_op jit(solution)/shard_map/ppermute | solution.py:416
  52.7 9.9 %collective-permute-start.14 = (bf16[96,576]{1,0:T(8,128)(2,1)}, bf16[96,576]{1,0:T(8,128)(2,1)}, u32[]{:S(2)}, u32[]{:S(2)}) collective-permute-start(bf16[96,576]{1,0:T(8,128)(2,1)} %fusion.54), channel_id=1, source_target_pairs={{8,0},{16,8},{24,16},{0,24},{40,32},{48,40},{56,48},{32,56},{72,64... | collective-permute-start | bytes 331784 | tf_op jit(solution)/shard_map/ppermute | solution.py:410
  62.6 1.5 collective-permute-done.7
  64.1 0.8 pad_maximum_fusion.4
  65.2 0.9 constant_dynamic-slice_fusion
  66.1 7.2 %collective-permute-done.14 = bf16[96,576]{1,0:T(8,128)(2,1)} collective-permute-done((bf16[96,576]{1,0:T(8,128)(2,1)}, bf16[96,576]{1,0:T(8,128)(2,1)}, u32[]{:S(2)}, u32[]{:S(2)}) %collective-permute-start.14) | collective-permute-done | bytes 110624 | tf_op jit(solution)/shard_map/ppermute | solution.py:410
  73.3 1.9 pad_maximum_fusion.3.rest_0_
  75.2 1.7 collective-permute-start.17
  76.9 0.5 collective-permute-start.18
  77.4 0.9 collective-permute-start.19
  78.3 0.3 collective-permute-start.11
  78.9 0.7 stack.77.info
  79.5 0.6 pad_add_fusion.token_ref
  80.1 0.7 fusion.33.fresh_ref
  80.9 5.2 %collective-permute-done.11 = bf16[256,576]{1,0:T(8,128)(2,1)} collective-permute-done((bf16[256,576]{1,0:T(8,128)(2,1)}, bf16[256,576]{1,0:T(8,128)(2,1)}, u32[]{:S(2)}, u32[]{:S(2)}) %collective-permute-start.11) | collective-permute-done | bytes 294944 | tf_op jit(solution)/shard_map/ppermute | solution.py:406
  86.0 9.0 %collective-permute-start.20 = (bf16[4,96,576]{2,1,0:T(8,128)(2,1)}, bf16[4,96,576]{2,1,0:T(8,128)(2,1)}, u32[]{:S(2)}, u32[]{:S(2)}) collective-permute-start(bf16[4,96,576]{2,1,0:T(8,128)(2,1)} %pad_maximum_fusion.3.rest_0_), channel_id=1, source_target_pairs={{0,1},{1,0},{2,3},{3,2},{4,5},{5,4},{6,7},{7,6},{8,9},{9,8},{10,11... | collective-permute-start | bytes 1327112 | tf_op jit(solution)/shard_map/ppermute | solution.py:402
  95.1 2.6 %pad_maximum_fusion.1.near_ref = bf16[4,256,576]{2,1,0:T(8,128)(2,1)} fusion(bf16[1,256,576]{2,1,0:T(8,128)(2,1)} %bitcast.30, bf16[1,256,576]{2,1,0:T(8,128)(2,1)} %bitcast.29, bf16[1,256,576]{2,1,0:T(8,128)(2,1)} %bitcast.28, bf16[1,256,576]{2,1,0:T(8,128)(2,1)} %bitcast.26), kind=kLoop, calls=%fused_computation.8 | loop fusion | flops 1769472 | bytes 2359296 | tf_op jit(solution)/shard_map/stack | solution.py:529
  97.7 2.4 %copy.42 = bf16[4,256,576]{1,2,0:T(8,128)(2,1)} copy(bf16[4,256,576]{2,1,0:T(8,128)(2,1)} %pad_maximum_fusion.1.near_ref) | data formatting | bytes 2359296 | tf_op jit(solution)/shard_map/stack | solution.py:529
  100.0 3.0 %collective-permute-start.13 = (bf16[4,256,576]{1,2,0:T(8,128)(2,1)}, bf16[4,256,576]{1,2,0:T(8,128)(2,1)}, u32[]{:S(2)}, u32[]{:S(2)}) collective-permute-start(bf16[4,256,576]{1,2,0:T(8,128)(2,1)} %copy.42), channel_id=1, source_target_pairs={{0,1},{1,0},{2,3},{3,2},{4,5},{5,4},{6,7},{7,6},{8,9},{9,8},{10,11... | collective-permute-start | bytes 3538952 | tf_op jit(solution)/shard_map/ppermute | solution.py:402
  103.1 0.4 collective-permute-start.22
  103.5 4.2 %collective-permute-done.19.rest_3_ = bf16[4,96,576]{2,1,0:T(8,128)(2,1)} collective-permute-done((bf16[4,96,576]{2,1,0:T(8,128)(2,1)}, bf16[4,96,576]{2,1,0:T(8,128)(2,1)}, u32[]{:S(2)}, u32[]{:S(2)}) %collective-permute-start.19) | collective-permute-done | bytes 442400 | tf_op jit(solution)/shard_map/ppermute | solution.py:416
  107.7 2.1 %collective-permute-start.23 = (bf16[4,96,576]{2,1,0:T(8,128)(2,1)}, bf16[4,96,576]{2,1,0:T(8,128)(2,1)}, u32[]{:S(2)}, u32[]{:S(2)}) collective-permute-start(bf16[4,96,576]{2,1,0:T(8,128)(2,1)} %collective-permute-done.19.rest_3_), channel_id=1, source_target_pairs={{0,1},{1,0},{2,3},{3,2},{4,5},{5,4},{6,7},{7,6},{8,9},{9,8},{10,11... | collective-permute-start | bytes 1327112 | tf_op jit(solution)/shard_map/ppermute | solution.py:402
  110.1 0.2 fusion.48.length
  110.3 0.6 convert_reduce_fusion.1
  111.7 0.8 select_reduce_fusion.order
  112.5 9.0 %attend_cache.1 = (bf16[32,32,512]{2,1,0:T(8,128)(2,1)}, bf16[32,32,128]{2,1,0:T(8,128)(2,1)}) custom-call(s32[32]{0:T(128)} %select_reduce_fusion.order, s32[32]{0:T(128)} %copy-done.7, s32[1]{0:T(128)} %bitcast.45.used, bf16[32,32,640]{2,1,0:T(8,128)(2,1)} %bitcast.100, bf16[32,576,384]{2,1,0:T(8,128)(2,1)} %bitcast.95, bf16[32,576,384]{2,1,0:T(8,128)(2,1)} %bitcast.96, ...), custom_call_target="tpu_custom_call" | custom-call | flops 3422552064 | bytes 14155776 | tf_op jit(solution)/shard_map/attend_cache/pallas_call | solution.py:347
  121.5 2.6 %fusion.23 = bf16[32,2,16,128]{3,0,1,2:T(8,128)(2,1)S(1)} fusion(bf16[16,512,128]{2,1,0:T(8,128)(2,1)S(1)} %copy-done, bf16[32,2,16,512]{3,2,1,0:T(8,128)(2,1)} %bitcast.104), kind=kOutput, calls=%fused_computation.13 | convolution fusion | flops 134348800 | bytes 3407872 | tf_op jit(solution)/shard_map/nshc,hcv->nshv/dot_general | solution.py:551
  124.1 0.2 copy.47
  124.3 0.9 pad_maximum_fusion.2
  125.1 7.3 %all-to-all-start.1 = ((bf16[16,64,256]{2,1,0:T(8,128)(2,1)}), bf16[16,64,256]{2,1,0:T(8,128)(2,1)S(1)}, u32[]{:S(2)}, u32[]{:S(2)}) async-start(bf16[16,64,256]{2,1,0:T(8,128)(2,1)} %pad_maximum_fusion.2), calls=%async_computation.1 | async-start | bytes 1048576 | tf_op jit(solution)/shard_map/all_to_all | solution.py:560
  132.4 2.4 %copy.43.far_ref = bf16[4,256,576]{2,1,0:T(8,128)(2,1)} copy(bf16[4,256,576]{1,2,0:T(8,128)(2,1)} %collective-permute-done.13) | data formatting | bytes 2359296 | tf_op jit(solution)/shard_map/ppermute | solution.py:402
  134.9 17.0 %attend_first.1 = (bf16[1,512,512]{2,1,0:T(8,128)(2,1)}, bf16[512,512]{1,0:T(8,128)(2,1)}, f32[512,128]{1,0:T(8,128)}) custom-call(s32[9]{0:T(128)} %stack.77.info, bf16[4,512,576]{2,1,0:T(8,128)(2,1)} %bitcast.126, bf16[512,576]{1,0:T(8,128)(2,1)} %bitcast.108, bf16[4,256,576]{2,1,0:T(8,128)(2,1)} %pad_maximum_fusion.1.near_ref, ...), custom_call_target="tpu_custom_call" | custom-call | flops 9730785280 | bytes 6635520 | tf_op jit(solution)/shard_map/attend_first/pallas_call | solution.py:238
  151.9 1.6 fusion.20
  153.5 0.9 copy.49
  154.3 0.8 copy-done.3
  155.1 3.0 %merge_decode.1 = bf16[16,32,128]{2,1,0:T(8,128)(2,1)} custom-call(s32[16]{0:T(128)} %copy-done.9, bf16[32,32,256]{2,1,0:T(8,128)(2,1)} %bitcast.103, f32[16,32,128]{2,1,0:T(8,128)} %bitcast.105, f32[16,32,128]{2,1,0:T(8,128)} %bitcast.116), custom_call_target="tpu_custom_call" | custom-call | tf_op jit(solution)/shard_map/merge_decode/pallas_call | solution.py:391
  158.1 22.2 %attend_later.1 = bf16[3,512,512]{2,1,0:T(8,128)(2,1)} custom-call(s32[9]{0:T(128)} %stack.77.info, bf16[4,512,576]{2,1,0:T(8,128)(2,1)} %bitcast.127, bf16[32,3,96,576]{3,2,1,0:T(8,128)(2,1)} %bitcast.125, bf16[4,256,576]{2,1,0:T(8,128)(2,1)} %pad_maximum_fusion.1.near_ref, bf16[4,256,576]{2,1,0:T(8,128)(2,1)} %copy.43.far_ref, s32[2,256]{1,0:T(2,128)} %pad_add_fusion.token_ref), custom_call_target="tpu_custom_call" | custom-call | flops 14092861440 | bytes 15925248 | tf_op jit(solution)/shard_map/attend_later/pallas_call | solution.py:202
  180.3 1.6 pad_maximum_fusion
  181.9 2.6 %fusion.12 = bf16[4,32,16,128]{3,1,0,2:T(8,128)(2,1)S(1)} fusion(bf16[16,512,128]{2,1,0:T(8,128)(2,1)S(1)} %copy-done, bf16[4,32,16,512]{3,2,1,0:T(8,128)(2,1)S(1)} %bitcast.102), kind=kOutput, calls=%fused_computation.10 | convolution fusion | flops 268697600 | bytes 4718592 | tf_op jit(solution)/shard_map/pthc,hcv->pthv/dot_general | solution.py:603
  184.5 1.1 copy.50
  (81 shorter events, 1.9 us)
Async XLA Ops:
  7.2 114.3 %copy-start = (bf16[16,512,128]{2,1,0:T(8,128)(2,1)S(1)}, bf16[16,512,128]{2,1,0:T(8,128)(2,1)}, u32[]{:S(2)}) copy-start(bf16[16,512,128]{2,1,0:T(8,128)(2,1)} %param.23) | copy-start | bytes 6291460
  7.2 10.8 %copy-start.2 = (bf16[896,576]{0,1:T(8,128)(2,1)S(1)}, bf16[896,576]{0,1:T(8,128)(2,1)}, u32[]{:S(2)}) copy-start(bf16[896,576]{0,1:T(8,128)(2,1)} %param.21) | copy-start | bytes 3096580
  7.2 150.9 %all-gather.3.cloned.1.call-start = ((), (), s32[]{:S(2)}) async-start(), calls=%async_computation.2 | async-start | bytes 12165120 | tf_op jit(solution)/shard_map/all_gather | solution.py:450
  7.2 12.5 %copy-start.6 = (s32[4]{0:T(128)S(1)}, s32[4]{0:T(128)}, u32[]{:S(2)}) copy-start(s32[4]{0:T(128)} %param.15) | copy-start | bytes 52
  7.3 13.7 %copy-start.10 = (s32[16]{0:T(128)S(1)}, s32[16]{0:T(128)}, u32[]{:S(2)}) copy-start(s32[16]{0:T(128)} %param.20) | copy-start | bytes 196
  7.3 14.5 %copy-start.11 = (s32[16,1]{0,1:T(1,128)S(1)}, s32[16,1]{0,1:T(1,128)}, u32[]{:S(2)}) copy-start(s32[16,1]{0,1:T(1,128)} %param.19) | copy-start | bytes 196
  10.8 55.3 %collective-permute-start.16 = (bf16[96,576]{1,0:T(8,128)(2,1)}, bf16[96,576]{1,0:T(8,128)(2,1)}, u32[]{:S(2)}, u32[]{:S(2)}) collective-permute-start(bf16[96,576]{1,0:T(8,128)(2,1)} %fusion.54), channel_id=1, source_target_pairs={{24,0},{0,8},{8,16},{16,24},{56,32},{32,40},{40,48},{48,56},{88,64... | collective-permute-start | bytes 331784 | tf_op jit(solution)/shard_map/ppermute | solution.py:410
  12.8 53.2 %collective-permute-start.15 = (bf16[96,576]{1,0:T(8,128)(2,1)}, bf16[96,576]{1,0:T(8,128)(2,1)}, u32[]{:S(2)}, u32[]{:S(2)}) collective-permute-start(bf16[96,576]{1,0:T(8,128)(2,1)} %fusion.54), channel_id=1, source_target_pairs={{16,0},{24,8},{0,16},{8,24},{48,32},{56,40},{32,48},{40,56},{80,64... | collective-permute-start | bytes 331784 | tf_op jit(solution)/shard_map/ppermute | solution.py:410
  17.9 12.0 %copy-start.8 = (f32[512]{0:T(512)S(1)}, f32[512]{0:T(512)}, u32[]{:S(2)}) copy-start(f32[512]{0:T(512)} %param.22) | copy-start | bytes 6148
  18.4 3.6 %collective-permute-start = (bf16[96,576]{1,0:T(8,128)(2,1)S(1)}, bf16[96,576]{1,0:T(8,128)(2,1)S(1)}, u32[]{:S(2)}, u32[]{:S(2)}) collective-permute-start(bf16[96,576]{1,0:T(8,128)(2,1)S(1)} %pad_maximum_fusion.5), channel_id=1, source_target_pairs={{0,1},{1,0},{2,3},{3,2},{4,5},{5,4},{6,7},{7,6},{8,9},{9,8},{10,11... | collective-permute-start | bytes 331784 | tf_op jit(solution)/shard_map/ppermute | solution.py:402
  22.0 13.8 %copy-start.9 = (s32[16]{0:T(128)}, s32[16]{0:T(128)S(1)}, u32[]{:S(2)}) copy-start(s32[16]{0:T(128)S(1)} %multiply_add_fusion.slot) | copy-start | bytes 196
  22.2 5.1 %collective-permute-start.3 = (bf16[48,576]{1,0:T(8,128)(2,1)S(1)}, bf16[48,576]{1,0:T(8,128)(2,1)S(1)}, u32[]{:S(2)}, u32[]{:S(2)}) collective-permute-start(bf16[48,576]{1,0:T(8,128)(2,1)S(1)} %get-tuple-element.32), channel_id=1, source_target_pairs={{6,0},{0,2},{2,4},{4,6},{7,1},{1,3},{3,5},{5,7},{14,8},{8,10},{10,... | collective-permute-start | bytes 165896 | tf_op jit(solution)/shard_map/ppermute | solution.py:406
  23.5 6.1 %collective-permute-start.2 = (bf16[48,576]{1,0:T(8,128)(2,1)S(1)}, bf16[48,576]{1,0:T(8,128)(2,1)S(1)}, u32[]{:S(2)}, u32[]{:S(2)}) collective-permute-start(bf16[48,576]{1,0:T(8,128)(2,1)S(1)} %get-tuple-element.31), channel_id=1, source_target_pairs={{4,0},{6,2},{0,4},{2,6},{5,1},{7,3},{1,5},{3,7},{12,8},{14,10},{8,... | collective-permute-start | bytes 165896 | tf_op jit(solution)/shard_map/ppermute | solution.py:406
  26.1 3.5 %collective-permute-start.1 = (bf16[48,576]{1,0:T(8,128)(2,1)S(1)}, bf16[48,576]{1,0:T(8,128)(2,1)S(1)}, u32[]{:S(2)}, u32[]{:S(2)}) collective-permute-start(bf16[48,576]{1,0:T(8,128)(2,1)S(1)} %get-tuple-element.30), channel_id=1, source_target_pairs={{2,0},{4,2},{6,4},{0,6},{3,1},{5,3},{7,5},{1,7},{10,8},{12,10},{14... | collective-permute-start | bytes 165896 | tf_op jit(solution)/shard_map/ppermute | solution.py:406
  30.1 12.9 %collective-permute-start.6 = (bf16[16,576]{1,0:T(8,128)(2,1)S(1)}, bf16[16,576]{1,0:T(8,128)(2,1)S(1)}, u32[]{:S(2)}, u32[]{:S(2)}) collective-permute-start(bf16[16,576]{1,0:T(8,128)(2,1)S(1)} %pad_maximum_fusion.11), channel_id=1, source_target_pairs={{24,0},{0,8},{8,16},{16,24},{56,32},{32,40},{40,48},{48,56},{88,64... | collective-permute-start | bytes 55304 | tf_op jit(solution)/shard_map/ppermute | solution.py:410
  30.2 12.9 %collective-permute-start.5 = (bf16[16,576]{1,0:T(8,128)(2,1)S(1)}, bf16[16,576]{1,0:T(8,128)(2,1)S(1)}, u32[]{:S(2)}, u32[]{:S(2)}) collective-permute-start(bf16[16,576]{1,0:T(8,128)(2,1)S(1)} %pad_maximum_fusion.11), channel_id=1, source_target_pairs={{16,0},{24,8},{0,16},{8,24},{48,32},{56,40},{32,48},{40,56},{80,64... | collective-permute-start | bytes 55304 | tf_op jit(solution)/shard_map/ppermute | solution.py:410
  32.5 10.6 %collective-permute-start.4 = (bf16[16,576]{1,0:T(8,128)(2,1)S(1)}, bf16[16,576]{1,0:T(8,128)(2,1)}, u32[]{:S(2)}, u32[]{:S(2)}) collective-permute-start(bf16[16,576]{1,0:T(8,128)(2,1)S(1)} %pad_maximum_fusion.11), channel_id=1, source_target_pairs={{8,0},{16,8},{24,16},{0,24},{40,32},{48,40},{56,48},{32,56},{72,64... | collective-permute-start | bytes 55304 | tf_op jit(solution)/shard_map/ppermute | solution.py:410
  35.8 74.1 %all-to-all-start = ((bf16[16,64,640]{2,1,0:T(8,128)(2,1)}), bf16[16,64,640]{2,1,0:T(8,128)(2,1)S(1)}, u32[]{:S(2)}, u32[]{:S(2)}) async-start(bf16[16,64,640]{2,1,0:T(8,128)(2,1)} %bitcast.101), calls=%async_computation | async-start | bytes 2621440 | tf_op jit(solution)/shard_map/all_to_all | solution.py:472
  43.8 8.9 %collective-permute-start.9 = (bf16[4,16,576]{2,1,0:T(8,128)(2,1)S(1)}, bf16[4,16,576]{2,1,0:T(8,128)(2,1)S(1)}, u32[]{:S(2)}, u32[]{:S(2)}) collective-permute-start(bf16[4,16,576]{2,1,0:T(8,128)(2,1)S(1)} %get-tuple-element.25), channel_id=1, source_target_pairs={{96,0},{104,8},{112,16},{120,24},{0,32},{8,40},{16,48},{24,56},{32... | collective-permute-start | bytes 221192 | tf_op jit(solution)/shard_map/ppermute | solution.py:416
  45.2 17.3 %collective-permute-start.8 = (bf16[4,16,576]{2,1,0:T(8,128)(2,1)S(1)}, bf16[4,16,576]{2,1,0:T(8,128)(2,1)S(1)}, u32[]{:S(2)}, u32[]{:S(2)}) collective-permute-start(bf16[4,16,576]{2,1,0:T(8,128)(2,1)S(1)} %get-tuple-element.25), channel_id=1, source_target_pairs={{64,0},{72,8},{80,16},{88,24},{96,32},{104,40},{112,48},{120,56},{... | collective-permute-start | bytes 221192 | tf_op jit(solution)/shard_map/ppermute | solution.py:416
  47.6 16.5 %collective-permute-start.7 = (bf16[4,16,576]{2,1,0:T(8,128)(2,1)S(1)}, bf16[4,16,576]{2,1,0:T(8,128)(2,1)S(1)}, u32[]{:S(2)}, u32[]{:S(2)}) collective-permute-start(bf16[4,16,576]{2,1,0:T(8,128)(2,1)S(1)} %get-tuple-element.25), channel_id=1, source_target_pairs={{32,0},{40,8},{48,16},{56,24},{64,32},{72,40},{80,48},{88,56},{96,... | collective-permute-start | bytes 221192 | tf_op jit(solution)/shard_map/ppermute | solution.py:416
  52.7 20.6 %collective-permute-start.14 = (bf16[96,576]{1,0:T(8,128)(2,1)}, bf16[96,576]{1,0:T(8,128)(2,1)}, u32[]{:S(2)}, u32[]{:S(2)}) collective-permute-start(bf16[96,576]{1,0:T(8,128)(2,1)} %fusion.54), channel_id=1, source_target_pairs={{8,0},{16,8},{24,16},{0,24},{40,32},{48,40},{56,48},{32,56},{72,64... | collective-permute-start | bytes 331784 | tf_op jit(solution)/shard_map/ppermute | solution.py:410
  64.9 13.7 %collective-permute-start.12 = (bf16[256,576]{1,0:T(8,128)(2,1)}, bf16[256,576]{1,0:T(8,128)(2,1)}, u32[]{:S(2)}, u32[]{:S(2)}) collective-permute-start(bf16[256,576]{1,0:T(8,128)(2,1)} %bitcast.27), channel_id=1, source_target_pairs={{6,0},{0,2},{2,4},{4,6},{7,1},{1,3},{3,5},{5,7},{14,8},{8,10},{10,... | collective-permute-start | bytes 884744 | tf_op jit(solution)/shard_map/ppermute | solution.py:406
  75.2 27.8 %collective-permute-start.17 = (bf16[4,96,576]{2,1,0:T(8,128)(2,1)}, bf16[4,96,576]{2,1,0:T(8,128)(2,1)}, u32[]{:S(2)}, u32[]{:S(2)}) collective-permute-start(bf16[4,96,576]{2,1,0:T(8,128)(2,1)} %pad_maximum_fusion.3.rest_0_), channel_id=1, source_target_pairs={{32,0},{40,8},{48,16},{56,24},{64,32},{72,40},{80,48},{88,56},{96,... | collective-permute-start | bytes 1327112 | tf_op jit(solution)/shard_map/ppermute | solution.py:416
  76.9 26.2 %collective-permute-start.18 = (bf16[4,96,576]{2,1,0:T(8,128)(2,1)}, bf16[4,96,576]{2,1,0:T(8,128)(2,1)}, u32[]{:S(2)}, u32[]{:S(2)}) collective-permute-start(bf16[4,96,576]{2,1,0:T(8,128)(2,1)} %pad_maximum_fusion.3.rest_0_), channel_id=1, source_target_pairs={{64,0},{72,8},{80,16},{88,24},{96,32},{104,40},{112,48},{120,56},{... | collective-permute-start | bytes 1327112 | tf_op jit(solution)/shard_map/ppermute | solution.py:416
  77.4 30.3 %collective-permute-start.19 = (bf16[4,96,576]{2,1,0:T(8,128)(2,1)}, bf16[4,96,576]{2,1,0:T(8,128)(2,1)}, u32[]{:S(2)}, u32[]{:S(2)}) collective-permute-start(bf16[4,96,576]{2,1,0:T(8,128)(2,1)} %pad_maximum_fusion.3.rest_0_), channel_id=1, source_target_pairs={{96,0},{104,8},{112,16},{120,24},{0,32},{8,40},{16,48},{24,56},{32... | collective-permute-start | bytes 1327112 | tf_op jit(solution)/shard_map/ppermute | solution.py:416
  78.3 7.7 %collective-permute-start.11 = (bf16[256,576]{1,0:T(8,128)(2,1)}, bf16[256,576]{1,0:T(8,128)(2,1)}, u32[]{:S(2)}, u32[]{:S(2)}) collective-permute-start(bf16[256,576]{1,0:T(8,128)(2,1)} %bitcast.27), channel_id=1, source_target_pairs={{4,0},{6,2},{0,4},{2,6},{5,1},{7,3},{1,5},{3,7},{12,8},{14,10},{8,... | collective-permute-start | bytes 884744 | tf_op jit(solution)/shard_map/ppermute | solution.py:406
  78.6 16.5 %collective-permute-start.10 = (bf16[256,576]{1,0:T(8,128)(2,1)}, bf16[256,576]{1,0:T(8,128)(2,1)}, u32[]{:S(2)}, u32[]{:S(2)}) collective-permute-start(bf16[256,576]{1,0:T(8,128)(2,1)} %bitcast.27), channel_id=1, source_target_pairs={{2,0},{4,2},{6,4},{0,6},{3,1},{5,3},{7,5},{1,7},{10,8},{12,10},{14... | collective-permute-start | bytes 884744 | tf_op jit(solution)/shard_map/ppermute | solution.py:406
  86.0 48.8 %collective-permute-start.20 = (bf16[4,96,576]{2,1,0:T(8,128)(2,1)}, bf16[4,96,576]{2,1,0:T(8,128)(2,1)}, u32[]{:S(2)}, u32[]{:S(2)}) collective-permute-start(bf16[4,96,576]{2,1,0:T(8,128)(2,1)} %pad_maximum_fusion.3.rest_0_), channel_id=1, source_target_pairs={{0,1},{1,0},{2,3},{3,2},{4,5},{5,4},{6,7},{7,6},{8,9},{9,8},{10,11... | collective-permute-start | bytes 1327112 | tf_op jit(solution)/shard_map/ppermute | solution.py:402
  100.0 32.4 %collective-permute-start.13 = (bf16[4,256,576]{1,2,0:T(8,128)(2,1)}, bf16[4,256,576]{1,2,0:T(8,128)(2,1)}, u32[]{:S(2)}, u32[]{:S(2)}) collective-permute-start(bf16[4,256,576]{1,2,0:T(8,128)(2,1)} %copy.42), channel_id=1, source_target_pairs={{0,1},{1,0},{2,3},{3,2},{4,5},{5,4},{6,7},{7,6},{8,9},{9,8},{10,11... | collective-permute-start | bytes 3538952 | tf_op jit(solution)/shard_map/ppermute | solution.py:402
  103.0 31.8 %collective-permute-start.21 = (bf16[4,96,576]{2,1,0:T(8,128)(2,1)}, bf16[4,96,576]{2,1,0:T(8,128)(2,1)}, u32[]{:S(2)}, u32[]{:S(2)}) collective-permute-start(bf16[4,96,576]{2,1,0:T(8,128)(2,1)} %collective-permute-done.17.rest_1_), channel_id=1, source_target_pairs={{0,1},{1,0},{2,3},{3,2},{4,5},{5,4},{6,7},{7,6},{8,9},{9,8},{10,11... | collective-permute-start | bytes 1327112 | tf_op jit(solution)/shard_map/ppermute | solution.py:402
  103.1 31.7 %collective-permute-start.22 = (bf16[4,96,576]{2,1,0:T(8,128)(2,1)}, bf16[4,96,576]{2,1,0:T(8,128)(2,1)}, u32[]{:S(2)}, u32[]{:S(2)}) collective-permute-start(bf16[4,96,576]{2,1,0:T(8,128)(2,1)} %collective-permute-done.18.rest_2_), channel_id=1, source_target_pairs={{0,1},{1,0},{2,3},{3,2},{4,5},{5,4},{6,7},{7,6},{8,9},{9,8},{10,11... | collective-permute-start | bytes 1327112 | tf_op jit(solution)/shard_map/ppermute | solution.py:402
  107.7 27.1 %collective-permute-start.23 = (bf16[4,96,576]{2,1,0:T(8,128)(2,1)}, bf16[4,96,576]{2,1,0:T(8,128)(2,1)}, u32[]{:S(2)}, u32[]{:S(2)}) collective-permute-start(bf16[4,96,576]{2,1,0:T(8,128)(2,1)} %collective-permute-done.19.rest_3_), channel_id=1, source_target_pairs={{0,1},{1,0},{2,3},{3,2},{4,5},{5,4},{6,7},{7,6},{8,9},{9,8},{10,11... | collective-permute-start | bytes 1327112 | tf_op jit(solution)/shard_map/ppermute | solution.py:402
  109.9 2.6 %copy-start.1 = (bf16[16,64,640]{2,1,0:T(8,128)(2,1)}, bf16[16,64,640]{2,1,0:T(8,128)(2,1)S(1)}, u32[]{:S(2)}) copy-start(bf16[16,64,640]{2,1,0:T(8,128)(2,1)S(1)} %all-to-all-done) | copy-start | bytes 3932164
  110.3 2.2 %copy-start.7 = (s32[32]{0:T(128)}, s32[32]{0:T(128)S(1)}, u32[]{:S(2)}) copy-start(s32[32]{0:T(128)S(1)} %fusion.48.length) | copy-start | bytes 388
  121.5 2.8 %copy-start.5 = (bf16[32,32,128]{2,1,0:T(8,128)(2,1)S(1)}, bf16[32,32,128]{2,1,0:T(8,128)(2,1)}, u32[]{:S(2)}) copy-start(bf16[32,32,128]{2,1,0:T(8,128)(2,1)} %get-tuple-element.9) | copy-start | bytes 786436
  125.1 29.2 %all-to-all-start.1 = ((bf16[16,64,256]{2,1,0:T(8,128)(2,1)}), bf16[16,64,256]{2,1,0:T(8,128)(2,1)S(1)}, u32[]{:S(2)}, u32[]{:S(2)}) async-start(bf16[16,64,256]{2,1,0:T(8,128)(2,1)} %pad_maximum_fusion.2), calls=%async_computation.1 | async-start | bytes 1048576 | tf_op jit(solution)/shard_map/all_to_all | solution.py:560
  154.3 0.8 copy-start.3
  158.1 22.2 %copy-start.4 = (bf16[1,512,512]{2,1,0:T(8,128)(2,1)S(1)}, bf16[1,512,512]{2,1,0:T(8,128)(2,1)}, u32[]{:S(2)}) copy-start(bf16[1,512,512]{2,1,0:T(8,128)(2,1)} %get-tuple-element.7) | copy-start | bytes 1572868
Sparse Core Ops, SparseCore 0:
  10.3 96.9 all-gather.2
